TPU v7x, 128 devices: a whole 4x4x4 slice. The times are simulated.
128 devices in a mesh: dp: 8 (over y_lo, x), ctx: 16 (over z, y_hi, core).
Axes of the slice: x: 4, y: 4 (y_hi: 2, y_lo: 2; y = y_hi * 2 + y_lo), z: 4, core: 2. Of those that a mesh axis runs over, the one named last changes fastest.
Arguments:
- hidden: bfloat16 [32768, 8192], P(('dp', 'ctx')), may hold values from -0.5 to 0.5
- queries: bfloat16 [32768, 512], P(('dp', 'ctx')), may hold values from -13 to 13
- key_rows: bfloat16 [32768, 128], P(('dp', 'ctx')), may hold values from -6 to 6
- value_rows: bfloat16 [32768, 128], P(('dp', 'ctx')), may hold values from -6 to 6
- out_grad: bfloat16 [32768, 512], P(('dp', 'ctx')), may hold values from -6 to 6
- doc_ids: int32 [32768], P(('dp', 'ctx')), may hold values from 4095 to 32767, as said below
- q_weight: bfloat16 [8192, 512], replicated, may hold values from -0.25 to 0.25
- k_weight: bfloat16 [8192, 128], replicated, may hold values from -0.5 to 0.5
- v_weight: bfloat16 [8192, 128], replicated, may hold values from -0.5 to 0.5
Outputs:
- input_grad: bfloat16 [32768, 8192], P(('dp', 'ctx'))
- kv_weight_grad: float32 [8192, 256], P(('dp', 'ctx'))
Inputs may be any that keep to these rules, and one draw needn't show every extreme that they name: `doc_ids`: A token's number is 4096 times its row along dp plus the index within that row of its document's last token; a document never leaves its row along dp.
All inputs are finite; a program needn't handle non-finite values.
Results may differ from a plain program's by a relative error of at most 0.0058.
Values may be sent and summed in bfloat16 or wider, within the bound.
A program may use at most 128 MiB of HBM per device.

v0:
```python
import jax
import jax.numpy as jnp
from jax import lax
from jax.sharding import PartitionSpec as P


def attend(query_pair, grad_pair, all_keys, all_values, allowed, score_scale):
    scores = (
        jnp.einsum("gtd,sd->gts", query_pair, all_keys, preferred_element_type=jnp.float32)
        * score_scale
    )
    scores = jnp.where(allowed[None], scores, -jnp.inf)
    row_max = jnp.max(scores, axis=2, keepdims=True)
    probs = jnp.exp(scores - row_max)
    probs = probs / jnp.sum(probs, axis=2, keepdims=True)
    probs_low = probs.astype(jnp.bfloat16)
    output = jnp.einsum("gts,sd->gtd", probs_low, all_values, preferred_element_type=jnp.float32)
    row_delta = jnp.sum(grad_pair.astype(jnp.float32) * output, axis=2, keepdims=True)
    value_grad = jnp.einsum("gts,gtd->sd", probs_low, grad_pair, preferred_element_type=jnp.float32)
    prob_grad = jnp.einsum("gtd,sd->gts", grad_pair, all_values, preferred_element_type=jnp.float32)
    score_grad = (score_scale * probs * (prob_grad - row_delta)).astype(jnp.bfloat16)
    query_grad = jnp.einsum("gts,sd->gtd", score_grad, all_keys, preferred_element_type=jnp.float32)
    key_grad = jnp.einsum("gts,gtd->sd", score_grad, query_pair, preferred_element_type=jnp.float32)
    return (query_grad, key_grad, value_grad)


def project_back(grad_rows, weight):
    return lax.dot_general(
        grad_rows, weight, (((1,), (1,)), ((), ())), preferred_element_type=jnp.float32
    )


def on_device(
    hidden, queries, key_rows, value_rows, out_grad, doc_ids, q_weight, k_weight, v_weight
):
    tok_rows = hidden.shape[0]
    head_size = key_rows.shape[1]
    head_count = queries.shape[1] // head_size
    score_scale = head_size ** (-0.5)
    all_keys, all_values, key_docs = (
        lax.all_gather(key_rows, "ctx", axis=0, tiled=True),
        lax.all_gather(value_rows, "ctx", axis=0, tiled=True),
        lax.all_gather(doc_ids, "ctx", axis=0, tiled=True),
    )
    key_count = all_keys.shape[0]
    query_pos = lax.axis_index("ctx") * tok_rows + jnp.arange(tok_rows, dtype=jnp.int32)
    key_pos = jnp.arange(key_count, dtype=jnp.int32)
    allowed = (doc_ids[:, None] == key_docs[None, :]) & (key_pos[None, :] <= query_pos[:, None])
    query_heads = queries.reshape(tok_rows, head_count, head_size).transpose(1, 0, 2)
    grad_heads = out_grad.reshape(tok_rows, head_count, head_size).transpose(1, 0, 2)
    query_parts = []
    key_term = jnp.zeros((key_count, head_size), jnp.float32)
    value_term = jnp.zeros((key_count, head_size), jnp.float32)
    for start_head in range(0, head_count, 2):
        query_piece, key_piece, value_piece = attend(
            query_heads[start_head : start_head + 2],
            grad_heads[start_head : start_head + 2],
            all_keys,
            all_values,
            allowed,
            score_scale,
        )
        query_parts.append(query_piece)
        key_term = key_term + key_piece
        value_term = value_term + value_piece
    query_grad = jnp.concatenate(query_parts, axis=0).transpose(1, 0, 2)
    query_grad = query_grad.reshape(tok_rows, head_count * head_size).astype(jnp.bfloat16)
    key_sum, value_sum = (
        lax.psum_scatter(key_term, "ctx", scatter_dimension=0, tiled=True),
        lax.psum_scatter(value_term, "ctx", scatter_dimension=0, tiled=True),
    )
    key_grad = key_sum.astype(jnp.bfloat16)
    value_grad = value_sum.astype(jnp.bfloat16)
    input_grad = project_back(query_grad, q_weight) + project_back(key_grad, k_weight)
    input_grad = (input_grad + project_back(value_grad, v_weight)).astype(jnp.bfloat16)
    kv_grads = jnp.concatenate([key_grad, value_grad], axis=1)
    kv_weight_grad = lax.psum_scatter(
        lax.dot_general(
            hidden, kv_grads, (((0,), (0,)), ((), ())), preferred_element_type=jnp.float32
        ),
        ("dp", "ctx"),
        scatter_dimension=0,
        tiled=True,
    )
    return (input_grad, kv_weight_grad)


def solution(mesh):
    return jax.shard_map(
        on_device,
        mesh=mesh,
        in_specs=(
            P(("dp", "ctx"), None),
            P(("dp", "ctx"), None),
            P(("dp", "ctx"), None),
            P(("dp", "ctx"), None),
            P(("dp", "ctx"), None),
            P(("dp", "ctx")),
            P(),
            P(),
            P(),
        ),
        out_specs=(P(("dp", "ctx"), None), P(("dp", "ctx"), None)),
        check_vma=False,
    )
```

profile of v0, /device:TPU:0, one launch (start us, length us, event | category | flops | bytes accessed | tf_op | source)
XLA Modules:
  0.0 956.3 jit_solution(16853349953576574823)
XLA Ops:
  7.2 0.0 copy-start
  7.2 0.0 all-gather.4.cloned.1.call-start
  7.2 0.7 all-gather.4.cloned.1.call-update
  7.9 0.0 all-gather.6.cloned.1.call-start
  8.0 0.7 all-gather.6.cloned.1.call-update
  8.7 0.0 reduce-scatter.6.cloned.1.call-start
  8.7 25.9 %all-gather = s32[16,1,256]{2,1,0:T(1,128)S(1)} all-gather(s32[1,1,256]{2,1,0:T(1,128)} %bitcast.103), channel_id=1, replica_groups=mesh['dp'=8,'ctx'=16] {'ctx'}, dimensions={0}, use_global_device_ids=true | all-gather | bytes 17408 | tf_op jit(solution)/shard_map/all_gather | solution.py:43
  34.7 3.0 fusion.11
  37.6 1.1 copy.37
  38.7 0.2 copy.38
  38.9 0.0 copy-start.10
  38.9 1.2 copy.39
  40.1 0.2 copy.40
  40.3 17.7 %all-gather.4.cloned.1.call-done = bf16[4096,128]{1,0:T(8,128)(2,1)} async-done(((bf16[256,128]{1,0:T(8,128)(2,1)}), bf16[4096,128]{1,0:T(8,128)(2,1)}) %all-gather.4.cloned.1.call-update) | async-done | bytes 1048592 | tf_op jit(solution)/shard_map/all_gather | solution.py:41
  58.0 7.8 fusion.60
  65.8 0.0 copy-done.10
  65.8 6.7 fusion.15
  72.5 31.6 %all-gather.6.cloned.1.call-done = bf16[4096,128]{1,0:T(8,128)(2,1)} async-done(((bf16[256,128]{1,0:T(8,128)(2,1)}), bf16[4096,128]{1,0:T(8,128)(2,1)}) %all-gather.6.cloned.1.call-update) | async-done | bytes 1048592 | tf_op jit(solution)/shard_map/all_gather | solution.py:42
  104.1 3.9 fusion.21
  108.0 0.0 copy-done.13
  108.0 0.0 copy-start.11
  108.0 4.5 multiply_convert_fusion
  112.5 0.0 copy-start.5
  112.6 0.0 copy-start.8
  112.6 1.9 copy-done.5
  114.5 0.0 copy-done.11
  114.5 2.7 convolution_bitcast_fusion.3
  117.2 0.0 copy-done.8
  117.2 7.7 fusion.65
  124.8 4.8 fusion.14
  129.6 0.0 copy-done.14
  129.6 0.0 copy-start.3
  129.6 1.3 fusion.20
  131.0 0.6 copy-done.7
  131.6 1.8 multiply_convert_fusion.1
  133.4 0.0 copy-done.3
  133.4 0.0 copy-start.1
  133.4 2.0 copy-done.1
  135.4 0.0 copy-done.6
  135.4 0.0 copy-done.12
  135.4 2.7 fusion.5
  138.0 0.0 reduce-scatter.6.cloned.1.call-update
  138.1 0.3 reduce-scatter.8.cloned.1.call-start
  138.3 0.0 copy-start.4
  138.3 3.6 convolution_bitcast_fusion.1
  142.0 0.0 copy-done.4
  142.0 2.6 fusion.6
  144.6 0.0 reduce-scatter.8.cloned.1.call-update
  144.6 0.0 reduce-scatter.10.cloned.1.call-start
  144.7 63.3 %reduce-scatter.6.cloned.1.call-done = f32[256,128]{1,0:T(8,128)} async-done(((f32[4096,128]{1,0:T(8,128)}), f32[256,128]{1,0:T(8,128)}) %reduce-scatter.6.cloned.1.call-update) | async-done | bytes 131088 | tf_op jit(solution)/shard_map/reduce_scatter | solution.py:69
  208.0 0.9 convert_element_type.42
  208.9 74.0 %reduce-scatter.8.cloned.1.call-done = f32[256,128]{1,0:T(8,128)} async-done(((f32[4096,128]{1,0:T(8,128)}), f32[256,128]{1,0:T(8,128)}) %reduce-scatter.8.cloned.1.call-update) | async-done | bytes 131088 | tf_op jit(solution)/shard_map/reduce_scatter | solution.py:70
  282.8 0.9 convert_element_type.43
  283.7 6.7 convolution_bitcast_fusion
  290.4 9.0 copy.66
  299.4 0.0 reduce-scatter.10.cloned.1.call-update
  299.5 3.8 convolution_convert_fusion
  303.3 1.5 convolution_convert_fusion.1
  304.9 5.8 fusion.70
  310.7 0.0 copy-start.9
  310.7 1.3 convolution_add_fusion.1
  312.1 0.2 copy-done.9
  312.3 3.3 fusion.2
  315.6 634.1 %reduce-scatter.10.cloned.1.call-done = f32[64,256]{1,0:T(8,128)} async-done(((f32[8192,256]{1,0:T(8,128)}), f32[64,256]{1,0:T(8,128)}) %reduce-scatter.10.cloned.1.call-update) | async-done | bytes 65552
  (10 shorter events, 0.0 us)
Async XLA Ops:
  7.2 303.6 %copy-start = (bf16[8192,128]{1,0:T(8,128)(2,1)S(1)}, bf16[8192,128]{1,0:T(8,128)(2,1)}, u32[]{:S(2)}) copy-start(bf16[8192,128]{1,0:T(8,128)(2,1)} %param.16) | copy-start | bytes 6291460
  7.2 50.8 %all-gather.4.cloned.1.call-start = ((), (), s32[]{:S(2)}) async-start(), calls=%async_computation.3 | async-start | bytes 1114112 | tf_op jit(solution)/shard_map/all_gather | solution.py:41
  7.9 96.2 %all-gather.6.cloned.1.call-start = ((), (), s32[]{:S(2)}) async-start(), calls=%async_computation.4 | async-start | bytes 1114112 | tf_op jit(solution)/shard_map/all_gather | solution.py:42
  8.7 199.3 %reduce-scatter.6.cloned.1.call-start = ((), (), s32[]{:S(2)}) async-start(), calls=%async_computation.5 | async-start | bytes 2228224 | tf_op jit(solution)/shard_map/reduce_scatter | solution.py:69
  38.9 26.9 %copy-start.10 = (bf16[256,4,128]{2,0,1:T(8,128)(2,1)}, bf16[256,4,128]{2,0,1:T(8,128)(2,1)S(1)}, u32[]{:S(2)}) copy-start(bf16[256,4,128]{2,0,1:T(8,128)(2,1)S(1)} %copy.38) | copy-start | bytes 786436
  104.1 3.9 copy-start.13
  108.0 6.5 copy-start.11
  112.5 1.9 copy-start.5
  112.6 4.6 copy-start.8
  124.8 4.8 copy-start.14
  124.8 6.8 copy-start.7
  129.6 3.7 copy-start.3
  131.6 3.8 copy-start.6
  131.6 3.8 copy-start.12
  133.4 2.0 copy-start.1
  138.1 144.8 %reduce-scatter.8.cloned.1.call-start = ((), (), s32[]{:S(2)}) async-start(), calls=%async_computation.6 | async-start | bytes 2228224 | tf_op jit(solution)/shard_map/reduce_scatter | solution.py:70
  138.3 3.6 copy-start.4
  144.6 805.1 %reduce-scatter.10.cloned.1.call-start = ((), (), s32[]{:S(2)}) async-start(), calls=%async_computation.7 | async-start | bytes 8454144
  299.4 3.9 copy-start.2
  310.7 1.6 copy-start.9
Sparse Core Ops, SparseCore 0:
  10.5 47.4 all-gather.3
  60.4 43.6 all-gather.5
  138.2 69.7 reduce-scatter.5
  212.8 70.0 reduce-scatter.7
  299.6 650.1 reduce-scatter.9
where the time goes:
time: 957 us; the launch traced here: 956 us
  waiting for transfers between devices  822 us (86%)
  matrix products  61.1 us (6%)
  blocking collectives  25.9 us (3%)
  local copies, waits for them, and re-layouts  16.4 us (2%)
  other arithmetic  16.3 us (2%)
  between operations  14 us (1%)
    unnamed x6, waiting for transfers between devices  636 us
    reduce_scatter x1, waiting for transfers between devices, on_device(): lax.psum_scatter(value_term, 'ctx', scatter_dimension=0, tiled=True)  74 us
    reduce_scatter x1, waiting for transfers between devices, on_device(): lax.psum_scatter(key_term, 'ctx', scatter_dimension=0, tiled=True)  63.3 us
    all_gather x1, waiting for transfers between devices, on_device(): lax.all_gather(value_rows, 'ctx', axis=0, tiled=True)  31.6 us
    all_gather x1, blocking collectives, on_device(): lax.all_gather(doc_ids, 'ctx', axis=0, tiled=True)  25.9 us
  transfers between devices with their start and end apart: 5, of which 5 were waited for; matrix products, arithmetic and copies ran while one was open for 5% of the time, Pallas kernels for 0%

commit v1 on v0

v1 whole, which is shorter than its diff:
```python
import functools

import jax
import jax.numpy as jnp
from jax import lax
from jax.experimental import pallas as pl
from jax.experimental.pallas import tpu as pltpu
from jax.sharding import PartitionSpec as P

MESH = pl.DeviceIdType.MESH
BF16 = jnp.bfloat16
F32 = jnp.float32
LOG2E = 1.4426950408889634
MASKED = -1e30


def dot(a, b):
    return jnp.dot(a, b, preferred_element_type=F32)


def attention_kernel(
    seq, q_ref, k_ref, v_ref, do_ref, docs_ref, dq_ref, dkv_ref,
    kv, q_t, do_t, probs, max_at, run_max, run_sum, out_t, delta, dq_t, acc,
    pair_out, pair_in, far_out, far_in,
    kv_send, kv_relay, kv_recv, pair_send, pair_recv, far_send, far_recv,
):
    tok, head = k_ref.shape
    heads = q_ref.shape[1] // head
    chips = kv.shape[0] // 2
    scale = head ** -0.5
    row = lax.axis_index("dp")
    me = lax.axis_index("ctx")
    chip, core = me // 2, me % 2
    other = 1 - core
    partner = chip * 2 + other

    def at(ctx):
        return (row, ctx)

    kv[me, 0:tok, 0:head] = k_ref[...]
    kv[me, 0:tok, head : 2 * head] = v_ref[...]
    last = docs_ref[...] - row * seq
    high, low = last // 64, last % 64
    digit = lax.broadcasted_iota(jnp.int32, (16, tok), 0)
    kv[me, tok : tok + 16, :] = jnp.where(digit == 0, high, low).astype(F32).astype(BF16)
    own_docs = last.astype(F32)

    barrier = pltpu.get_barrier_semaphore()
    for step in range(1, chips):
        peer = lax.rem(chip + step, chips) * 2 + core
        pl.semaphore_signal(barrier, inc=1, device_id=at(peer), device_id_type=MESH)
    pl.semaphore_signal(barrier, inc=1, device_id=at(partner), device_id_type=MESH)
    pl.semaphore_wait(barrier, chips)

    def kv_copy(slot, send_sem, target):
        return pltpu.make_async_remote_copy(
            src_ref=kv.at[slot], dst_ref=kv.at[slot], send_sem=send_sem,
            recv_sem=kv_recv.at[slot], device_id=at(target), device_id_type=MESH)

    def pair_copy(index):
        return pltpu.make_async_remote_copy(
            src_ref=pair_out.at[index], dst_ref=pair_in.at[index], send_sem=pair_send.at[index],
            recv_sem=pair_recv.at[index], device_id=at(partner), device_id_type=MESH)

    def far_copy(index, slot):
        return pltpu.make_async_remote_copy(
            src_ref=far_out.at[index], dst_ref=far_in.at[slot], send_sem=far_send.at[index],
            recv_sem=far_recv.at[slot], device_id=at(index * 2 + core), device_id_type=MESH)

    @pl.when(core == 0)
    def _():
        kv_copy(me, kv_send.at[chip], partner).start()

    @pl.loop(chip + 1, chips)
    def _(target):
        kv_copy(me, kv_send.at[target], target * 2 + core).start()

    for h in range(heads):
        cols = slice(h * head, (h + 1) * head)
        rows = slice(h * tok, (h + 1) * tok)
        q_t[:, rows] = q_ref[:, cols].T
        do_t[:, rows] = do_ref[:, cols].T
    run_max[...] = jnp.full_like(run_max, MASKED)
    run_sum[...] = jnp.zeros_like(run_sum)
    out_t[...] = jnp.zeros_like(out_t)
    dq_t[...] = jnp.zeros_like(dq_t)

    @pl.loop(0, 2 * (chip + 1))
    def _(i):
        back, second = i // 2, i % 2
        source = chip - back
        slot = 2 * source + jnp.where(second == 0, core, other)
        skipped = (i == 1) & (core == 0)

        @pl.when((i > 0) & jnp.logical_not(skipped))
        def _():
            kv_copy(slot, kv_relay.at[source], partner).wait_recv()

        @pl.when((i > 0) & (second == 0))
        def _():
            kv_copy(slot, kv_relay.at[source], partner).start()

        @pl.when(jnp.logical_not(skipped))
        def _():
            keys = kv[slot, 0:tok, 0:head]
            values_t = kv[slot, 0:tok, head : 2 * head].T
            digits = kv[slot, tok : tok + 16, :].astype(F32)
            key_docs = digits[0:1, :] * 64.0 + digits[1:2, :]
            key_docs = jnp.broadcast_to(key_docs, (tok, tok)).T
            key_pos = lax.broadcasted_iota(jnp.int32, (tok, tok), 0)
            query_pos = lax.broadcasted_iota(jnp.int32, (tok, tok), 1)
            allowed = (key_docs == own_docs) & (key_pos - query_pos <= (me - slot) * tok)
            for h in range(heads):
                rows = slice(h * tok, (h + 1) * tok)
                scores = dot(keys, q_t[:, rows]) * (scale * LOG2E)
                scores = jnp.where(allowed, scores, MASKED)
                old_max = run_max[:, rows]
                new_max = jnp.maximum(old_max, jnp.max(scores, axis=0, keepdims=True))
                weights = jnp.exp2(scores - new_max)
                shrink = jnp.exp2(old_max - new_max)
                run_max[:, rows] = new_max
                max_at[slot, :, rows] = new_max
                run_sum[:, rows] = run_sum[:, rows] * shrink + jnp.sum(weights, axis=0, keepdims=True)
                probs[slot, :, rows] = weights
                out_t[:, rows] = out_t[:, rows] * shrink + dot(values_t, weights.astype(BF16))

    run_sum[...] = 1.0 / run_sum[...]
    delta[...] = run_sum[...] * jnp.sum(out_t[...] * do_t[...].astype(F32), axis=0, keepdims=True)

    @pl.loop(0, 2 * (chip + 1))
    def _(i):
        source, second = i // 2, i % 2
        slot = 2 * source + jnp.where(second == 0, other, core)
        own_chip = source == chip
        skipped = own_chip & (second == 0) & (core == 0)

        @pl.when(jnp.logical_not(skipped))
        def _():
            keys_t = kv[slot, 0:tok, 0:head].T
            values = kv[slot, 0:tok, head : 2 * head]
            key_part = jnp.zeros((tok, head), F32)
            value_part = jnp.zeros((tok, head), F32)
            for h in range(heads):
                cols = slice(h * head, (h + 1) * head)
                rows = slice(h * tok, (h + 1) * tok)
                factor = jnp.exp2(max_at[slot, :, rows] - run_max[:, rows]) * run_sum[:, rows]
                prob = probs[slot, :, rows] * factor
                prob_grad = dot(values, do_t[:, rows])
                score_grad = (scale * prob * (prob_grad - delta[:, rows])).astype(BF16)
                value_part += dot(prob.astype(BF16), do_ref[:, cols])
                key_part += dot(score_grad, q_ref[:, cols])
                dq_t[:, rows] += dot(keys_t, score_grad)
            acc[:, 0:head] = key_part
            acc[:, head : 2 * head] = value_part

        @pl.when((second == 0) & jnp.logical_not(skipped))
        def _():
            pair_out[source] = acc[...].astype(BF16)
            pair_copy(source).start()

        @pl.when((second == 1) & jnp.logical_not(own_chip))
        def _():
            pair_copy(source).wait_recv()
            far_out[source] = (acc[...] + pair_in[source].astype(F32)).astype(BF16)
            far_copy(source, chip).start()

    for h in range(heads):
        cols = slice(h * head, (h + 1) * head)
        rows = slice(h * tok, (h + 1) * tok)
        dq_ref[:, cols] = dq_t[:, rows].T.astype(BF16)

    @pl.when(core == 0)
    def _():
        pair_copy(chip).wait_recv()
        acc[...] += pair_in[chip].astype(F32)

    @pl.loop(chip + 1, chips)
    def _(source):
        far_copy(source, source).wait_recv()
        acc[...] += far_in[source].astype(F32)

    dkv_ref[...] = acc[...].astype(BF16)

    @pl.when(core == 0)
    def _():
        kv_copy(me, kv_send.at[chip], partner).wait_send()

    @pl.when(core == 1)
    def _():
        pair_copy(chip).wait_send()

    @pl.loop(chip + 1, chips)
    def _(target):
        kv_copy(me, kv_send.at[target], target * 2 + core).wait_send()

    @pl.loop(0, chip)
    def _(source):
        kv_copy(2 * source + core, kv_relay.at[source], partner).wait_send()
        pair_copy(source).wait_send()
        far_copy(source, chip).wait_send()


def attention_grads(queries, key_rows, value_rows, out_grad, docs, n_ctx):
    tok, head = key_rows.shape
    width = queries.shape[1]
    heads = width // head
    chips = n_ctx // 2
    vmem = pl.BlockSpec(memory_space=pltpu.VMEM)
    dma = pltpu.SemaphoreType.DMA
    return pl.pallas_call(
        functools.partial(attention_kernel, tok * n_ctx),
        out_shape=(
            jax.ShapeDtypeStruct((tok, width), BF16),
            jax.ShapeDtypeStruct((tok, 2 * head), BF16),
        ),
        in_specs=[vmem] * 5,
        out_specs=(vmem, vmem),
        scratch_shapes=[
            pltpu.VMEM((n_ctx, tok + 16, 2 * head), BF16),
            pltpu.VMEM((head, heads * tok), BF16),
            pltpu.VMEM((head, heads * tok), BF16),
            pltpu.VMEM((n_ctx, tok, heads * tok), F32),
            pltpu.VMEM((n_ctx, 1, heads * tok), F32),
            pltpu.VMEM((1, heads * tok), F32),
            pltpu.VMEM((1, heads * tok), F32),
            pltpu.VMEM((head, heads * tok), F32),
            pltpu.VMEM((1, heads * tok), F32),
            pltpu.VMEM((head, heads * tok), F32),
            pltpu.VMEM((tok, 2 * head), F32),
            pltpu.VMEM((chips, tok, 2 * head), BF16),
            pltpu.VMEM((chips, tok, 2 * head), BF16),
            pltpu.VMEM((chips, tok, 2 * head), BF16),
            pltpu.VMEM((chips, tok, 2 * head), BF16),
            dma((chips,)), dma((chips,)), dma((n_ctx,)),
            dma((chips,)), dma((chips,)), dma((chips,)), dma((chips,)),
        ],
        compiler_params=pltpu.CompilerParams(
            collective_id=0, has_side_effects=True, vmem_limit_bytes=56 * 1024 * 1024
        ),
    )(queries, key_rows, value_rows, out_grad, docs)


def project_back(grad_rows, weight):
    return lax.dot_general(
        grad_rows, weight, (((1,), (1,)), ((), ())), preferred_element_type=F32
    )


def on_device(
    n_ctx, hidden, queries, key_rows, value_rows, out_grad, doc_ids, q_weight, k_weight, v_weight
):
    head = key_rows.shape[1]
    query_grad, kv_grads = attention_grads(
        queries, key_rows, value_rows, out_grad, doc_ids.reshape(1, -1), n_ctx)
    key_grad, value_grad = kv_grads[:, :head], kv_grads[:, head:]
    input_grad = project_back(query_grad, q_weight) + project_back(key_grad, k_weight)
    input_grad = (input_grad + project_back(value_grad, v_weight)).astype(BF16)
    kv_weight_grad = lax.psum_scatter(
        lax.dot_general(hidden, kv_grads, (((0,), (0,)), ((), ())), preferred_element_type=F32),
        ("dp", "ctx"),
        scatter_dimension=0,
        tiled=True,
    )
    return (input_grad, kv_weight_grad)


def solution(mesh):
    tokens = P(("dp", "ctx"), None)
    return jax.shard_map(
        functools.partial(on_device, mesh.shape["ctx"]),
        mesh=mesh,
        in_specs=(tokens, tokens, tokens, tokens, tokens, P(("dp", "ctx")), P(), P(), P()),
        out_specs=(tokens, tokens),
        check_vma=False,
    )
```

time: 957 us -> 733 us (0.77)
  waiting for transfers between devices: 822 us -> 648 us
  matrix products: 61.1 us -> 17.1 us
  Pallas kernels: 0 us -> 44 us
  blocking collectives: 25.9 us -> 0 us
  other arithmetic: 16.3 us -> 0 us
    reduce_scatter x2 -> x0, waiting for transfers between devices: 137 us -> none  [the longest x1 74 us: on_device(): lax.psum_scatter(value_term, 'ctx', scatter_dimension=0, tiled=True)]
    all_gather x2 -> x0, waiting for transfers between devices: 49.3 us -> none  [the longest x1 31.6 us: on_device(): lax.all_gather(value_rows, 'ctx', axis=0, tiled=True)]
    pallas_call x0 -> x1, Pallas kernels: none -> 44 us  [attention_grads(): pl.pallas_call(functools.partial(attention_kernel, tok * n_ctx), out_shap...]
    dot_general x10 -> x0, matrix products: 28.4 us -> none  [the longest x2 6.28 us: attend(): jnp.einsum('gtd,sd->gts', grad_pair, all_values, preferred_element_type=j...]
    all_gather x1 -> x0, blocking collectives: 25.9 us -> none  [on_device(): lax.all_gather(doc_ids, 'ctx', axis=0, tiled=True)]
    sub x2 -> x0, matrix products: 15.5 us -> none  [attend(): probs = jnp.exp(scores - row_max)]
    convert_element_type x4 -> x0, other arithmetic: 13.3 us -> none  [the longest x2 11.5 us: attend(): probs_low = probs.astype(jnp.bfloat16)]
    unnamed x6 -> x2, waiting for transfers between devices: 636 us -> 648 us
  transfers between devices with their start and end apart: 5 -> 1, of which waited for: 5 -> 1; matrix products, arithmetic and copies ran while one was open for 5% -> 1% of each run, Pallas kernels for 0% -> 0%
where the time goes in v1:
time: 733 us
  waiting for transfers between devices  648 us (88%)
  Pallas kernels  44 us (6%)
  matrix products  17.1 us (2%)
  between operations  14.1 us (2%)
  local copies, waits for them, and re-layouts  10.2 us (1%)
    unnamed x2, waiting for transfers between devices  648 us
    pallas_call x1, Pallas kernels, attention_grads(): pl.pallas_call(functools.partial(attention_kernel, tok * n_ctx), out_shap...  44 us
  transfers between devices with their start and end apart: 1, of which 1 were waited for; matrix products, arithmetic and copies ran while one was open for 1% of the time, Pallas kernels for 0%

profile of v1, /device:TPU:0, one launch (start us, length us, event | category | flops | bytes accessed | tf_op | source)
XLA Modules:
  0.0 733.1 jit_solution(1544795903351339054)
XLA Ops:
  7.2 0.0 copy-start
  7.2 0.0 reduce-scatter.4.cloned.1.call-start
  7.2 44.0 %shard_map.104 = (bf16[256,512]{1,0:T(8,128)(2,1)}, bf16[256,256]{1,0:T(8,128)(2,1)}) custom-call(bf16[256,512]{1,0:T(8,128)(2,1)} %q_ref.1, bf16[256,128]{1,0:T(8,128)(2,1)} %k_ref.1, bf16[256,128]{1,0:T(8,128)(2,1)} %v_ref.1, bf16[256,512]{1,0:T(8,128)(2,1)} %do_ref.1, s32[1,256]{1,0:T(1,128)} %bitcast.10), custom_call_target="tpu_custom_call" | custom-call | tf_op jit(solution)/shard_map/pallas_call | solution.py:210
  51.2 6.8 convolution_bitcast_fusion
  58.0 9.0 %copy.13 = f32[8192,256]{1,0:T(8,128)} copy(f32[8192,256]{0,1:T(8,128)} %convolution_bitcast_fusion) | data formatting | bytes 16777216
  67.0 0.0 copy-start.3
  67.0 0.0 reduce-scatter.4.cloned.1.call-update
  67.0 0.9 copy-done.3
  67.9 0.0 copy-start.2
  67.9 5.8 fusion.3
  73.7 0.0 copy-done
  73.7 0.0 copy-done.2
  73.7 0.0 copy-start.1
  73.7 1.3 convolution_add_fusion.1
  75.0 0.3 copy-done.1
  75.3 3.3 fusion
  78.6 647.7 %reduce-scatter.4.cloned.1.call-done = f32[64,256]{1,0:T(8,128)} async-done(((f32[8192,256]{1,0:T(8,128)}), f32[64,256]{1,0:T(8,128)}) %reduce-scatter.4.cloned.1.call-update) | async-done | bytes 65552
Async XLA Ops:
  7.2 66.6 %copy-start = (bf16[8192,128]{1,0:T(8,128)(2,1)S(1)}, bf16[8192,128]{1,0:T(8,128)(2,1)}, u32[]{:S(2)}) copy-start(bf16[8192,128]{1,0:T(8,128)(2,1)} %param.16) | copy-start | bytes 6291460
  7.2 719.1 %reduce-scatter.4.cloned.1.call-start = ((), (), s32[]{:S(2)}) async-start(), calls=%async_computation.1 | async-start | bytes 8454144
  67.0 0.9 copy-start.3
  67.9 5.8 copy-start.2
  73.7 1.6 copy-start.1
Sparse Core Ops, SparseCore 0:
  67.1 659.1 reduce-scatter.3

commit v2 on v1

--- a/solution.py
+++ b/solution.py
@@ -18,11 +18,21 @@
     return jnp.dot(a, b, preferred_element_type=F32)
 
 
-def attention_kernel(
-    seq, q_ref, k_ref, v_ref, do_ref, docs_ref, dq_ref, dkv_ref,
+def dot_rows(a, b):
+    return lax.dot_general(a, b, (((1,), (1,)), ((), ())), preferred_element_type=F32)
+
+
+def backward_kernel(
+    seq, q_ref, k_ref, v_ref, do_ref, docs_ref, hidden_ref, qw_ref, kw_ref, vw_ref,
+    grad_ref, wgrad_ref,
     kv, q_t, do_t, probs, max_at, run_max, run_sum, out_t, delta, dq_t, acc,
     pair_out, pair_in, far_out, far_in,
+    wide, hidden_t, hidden_in, qw, kw, vw, dq, dkv,
+    sum1_x, sum1_y, sum1_z, got1_x, got1_y, got1_z,
+    sum2_x, sum2_y, sum2_z, got2_x, got2_y, got2_z,
+    sum3_x, sum3_y, sum3_z, got3_x, got3_y, got3_z,
     kv_send, kv_relay, kv_recv, pair_send, pair_recv, far_send, far_recv,
+    load_sem, store_sem, core_send, core_recv, ring_send, ring_recv,
 ):
     tok, head = k_ref.shape
     heads = q_ref.shape[1] // head
@@ -33,9 +43,22 @@
     chip, core = me // 2, me % 2
     other = 1 - core
     partner = chip * 2 + other
+    place = (row % 4, (chip % 2) * 2 + row // 4, chip // 2)
 
     def at(ctx):
         return (row, ctx)
+
+    def along(axis, step):
+        x, y, z = [lax.rem(p + step, 4) if i == axis else p for i, p in enumerate(place)]
+        return ((y % 2) * 4 + x, z * 4 + (y // 2) * 2 + core)
+
+    loads = [
+        pltpu.make_async_copy(src, dst, load_sem.at[i])
+        for i, (src, dst) in enumerate(
+            ((hidden_ref, wide), (qw_ref, qw), (kw_ref, kw), (vw_ref, vw)))
+    ]
+    for load in loads:
+        load.start()
 
     kv[me, 0:tok, 0:head] = k_ref[...]
     kv[me, 0:tok, head : 2 * head] = v_ref[...]
@@ -50,7 +73,9 @@
         peer = lax.rem(chip + step, chips) * 2 + core
         pl.semaphore_signal(barrier, inc=1, device_id=at(peer), device_id_type=MESH)
     pl.semaphore_signal(barrier, inc=1, device_id=at(partner), device_id_type=MESH)
-    pl.semaphore_wait(barrier, chips)
+    for axis, step in ((0, 1), (0, 2), (0, 3), (1, 1), (1, 3)):
+        pl.semaphore_signal(barrier, inc=1, device_id=along(axis, step), device_id_type=MESH)
+    pl.semaphore_wait(barrier, chips + 5)
 
     def kv_copy(slot, send_sem, target):
         return pltpu.make_async_remote_copy(
@@ -84,6 +109,19 @@
     run_sum[...] = jnp.zeros_like(run_sum)
     out_t[...] = jnp.zeros_like(out_t)
     dq_t[...] = jnp.zeros_like(dq_t)
+
+    loads[0].wait()
+
+    @pl.loop(0, hidden_t.shape[0])
+    def _(group):
+        turned = wide[:, pl.ds(pl.multiple_of(group * 128, 128), 128)].T
+        hidden_t[group, 0] = turned[0:64]
+        hidden_t[group, 1] = turned[64:128]
+
+    hidden_copy = pltpu.make_async_remote_copy(
+        src_ref=hidden_t.at[:, other], dst_ref=hidden_in, send_sem=core_send.at[0],
+        recv_sem=core_recv.at[0], device_id=at(partner), device_id_type=MESH)
+    hidden_copy.start()
 
     @pl.loop(0, 2 * (chip + 1))
     def _(i):
@@ -167,7 +205,7 @@
     for h in range(heads):
         cols = slice(h * head, (h + 1) * head)
         rows = slice(h * tok, (h + 1) * tok)
-        dq_ref[:, cols] = dq_t[:, rows].T.astype(BF16)
+        dq[:, cols] = dq_t[:, rows].T.astype(BF16)
 
     @pl.when(core == 0)
     def _():
@@ -179,7 +217,88 @@
         far_copy(source, source).wait_recv()
         acc[...] += far_in[source].astype(F32)
 
-    dkv_ref[...] = acc[...].astype(BF16)
+    dkv[0] = acc[...].astype(BF16)
+    dkv_copy = pltpu.make_async_remote_copy(
+        src_ref=dkv.at[0], dst_ref=dkv.at[1], send_sem=core_send.at[1],
+        recv_sem=core_recv.at[1], device_id=at(partner), device_id_type=MESH)
+    dkv_copy.start()
+
+    orders = ((0, 1, 2), (1, 2, 0), (2, 0, 1))
+    sums = ((sum1_x, sum1_y, sum1_z), (sum2_x, sum2_y, sum2_z), (sum3_x, sum3_y, sum3_z))
+    gots = ((got1_x, got1_y, got1_z), (got2_x, got2_y, got2_z), (got3_x, got3_y, got3_z))
+
+    def ring_copy(stage, part, step):
+        axis = orders[part][stage]
+        return pltpu.make_async_remote_copy(
+            src_ref=sums[stage][part].at[lax.rem(place[axis] + step, 4)],
+            dst_ref=gots[stage][part].at[step - 1],
+            send_sem=ring_send.at[stage, part, step - 1],
+            recv_sem=ring_recv.at[stage, part, step - 1],
+            device_id=along(axis, step), device_id_type=MESH)
+
+    hidden_copy.wait_recv()
+    dkv_copy.wait_recv()
+    for step in (2, 1, 3, 0):
+        x = lax.rem(place[0] + step, 4)
+        for y_lo in range(2):
+            groups = pl.ds(y_lo * 32 + x * 8, 8)
+            own = hidden_t[groups, core].reshape(512, tok)
+            paired = hidden_in[groups].reshape(512, tok)
+            terms = (dot(own, dkv[0]) + dot(paired, dkv[1])).astype(BF16).reshape(4, 2, 64, 2 * head)
+            for y_hi in range(2):
+                y = y_hi * 2 + y_lo
+                sum1_x[x, y] = terms[:, y_hi, 0:48, 0:head]
+                sum1_y[y, :, x] = terms[:, y_hi, 0:48, head : 2 * head]
+                sum1_z[:, x, y] = terms[:, y_hi, 48:64, :]
+        if step > 0:
+            ring_copy(0, 0, step).start()
+    for part in (1, 2):
+        for step in (2, 1, 3):
+            ring_copy(0, part, step).start()
+
+    for load in loads[1:]:
+        load.wait()
+    tile = 512
+
+    def store_copy(index):
+        cols = pl.ds(pl.multiple_of(index * tile, tile), tile)
+        return pltpu.make_async_copy(wide.at[:, cols], grad_ref.at[:, cols], store_sem.at[index])
+
+    @pl.loop(0, store_sem.shape[0])
+    def _(index):
+        rows = pl.ds(pl.multiple_of(index * tile, tile), tile)
+        total = dot_rows(dq[...], qw[rows, :])
+        total += dot_rows(dkv[0, :, 0:head], kw[rows, :])
+        total += dot_rows(dkv[0, :, head : 2 * head], vw[rows, :])
+        wide[:, rows] = total.astype(BF16)
+        store_copy(index).start()
+
+    for stage in range(3):
+        for part in range(3):
+            for step in (1, 3, 2):
+                ring_copy(stage, part, step).wait_recv()
+            mine = place[orders[part][stage]]
+            total = sums[stage][part][mine].astype(F32)
+            for step in range(3):
+                total += gots[stage][part][step].astype(F32)
+            if stage < 2:
+                sums[stage + 1][part][...] = total.astype(sums[stage + 1][part].dtype)
+                for step in (2, 1, 3):
+                    ring_copy(stage + 1, part, step).start()
+            else:
+                wgrad_ref[(slice(0, 48), slice(0, 48), slice(48, 64))[part],
+                          (slice(0, head), slice(head, 2 * head), slice(0, 2 * head))[part]] = total
+
+    hidden_copy.wait_send()
+    dkv_copy.wait_send()
+    for stage in range(3):
+        for part in range(3):
+            for step in (1, 2, 3):
+                ring_copy(stage, part, step).wait_send()
+
+    @pl.loop(0, store_sem.shape[0])
+    def _(index):
+        store_copy(index).wait()
 
     @pl.when(core == 0)
     def _():
@@ -200,21 +319,30 @@
         far_copy(source, chip).wait_send()
 
 
-def attention_grads(queries, key_rows, value_rows, out_grad, docs, n_ctx):
+def on_device(
+    n_ctx, hidden, queries, key_rows, value_rows, out_grad, doc_ids, q_weight, k_weight, v_weight
+):
     tok, head = key_rows.shape
     width = queries.shape[1]
+    model = hidden.shape[1]
     heads = width // head
     chips = n_ctx // 2
     vmem = pl.BlockSpec(memory_space=pltpu.VMEM)
+    hbm = pl.BlockSpec(memory_space=pl.ANY)
     dma = pltpu.SemaphoreType.DMA
+    sums = []
+    for lead in ((4, 4, 4), (4, 4), (4,)):
+        for first in (lead, (3,) + lead[1:]):
+            for block in ((48, head), (48, head), (16, 2 * head)):
+                sums.append(pltpu.VMEM(first + block, BF16))
     return pl.pallas_call(
-        functools.partial(attention_kernel, tok * n_ctx),
+        functools.partial(backward_kernel, tok * n_ctx),
         out_shape=(
-            jax.ShapeDtypeStruct((tok, width), BF16),
-            jax.ShapeDtypeStruct((tok, 2 * head), BF16),
+            jax.ShapeDtypeStruct((tok, model), BF16),
+            jax.ShapeDtypeStruct((64, 2 * head), F32),
         ),
-        in_specs=[vmem] * 5,
-        out_specs=(vmem, vmem),
+        in_specs=[vmem] * 5 + [hbm] * 4,
+        out_specs=(hbm, vmem),
         scratch_shapes=[
             pltpu.VMEM((n_ctx, tok + 16, 2 * head), BF16),
             pltpu.VMEM((head, heads * tok), BF16),
@@ -231,37 +359,24 @@
             pltpu.VMEM((chips, tok, 2 * head), BF16),
             pltpu.VMEM((chips, tok, 2 * head), BF16),
             pltpu.VMEM((chips, tok, 2 * head), BF16),
+            pltpu.VMEM((tok, model), BF16),
+            pltpu.VMEM((model // 128, 2, 64, tok), BF16),
+            pltpu.VMEM((model // 128, 64, tok), BF16),
+            pltpu.VMEM((model, width), BF16),
+            pltpu.VMEM((model, head), BF16),
+            pltpu.VMEM((model, head), BF16),
+            pltpu.VMEM((tok, width), BF16),
+            pltpu.VMEM((2, tok, 2 * head), BF16),
+        ] + sums + [
             dma((chips,)), dma((chips,)), dma((n_ctx,)),
             dma((chips,)), dma((chips,)), dma((chips,)), dma((chips,)),
+            dma((4,)), dma((model // 512,)), dma((2,)), dma((2,)), dma((3, 3, 3)), dma((3, 3, 3)),
         ],
         compiler_params=pltpu.CompilerParams(
-            collective_id=0, has_side_effects=True, vmem_limit_bytes=56 * 1024 * 1024
+            collective_id=0, has_side_effects=True, vmem_limit_bytes=60 * 1024 * 1024
         ),
-    )(queries, key_rows, value_rows, out_grad, docs)
-
-
-def project_back(grad_rows, weight):
-    return lax.dot_general(
-        grad_rows, weight, (((1,), (1,)), ((), ())), preferred_element_type=F32
-    )
-
-
-def on_device(
-    n_ctx, hidden, queries, key_rows, value_rows, out_grad, doc_ids, q_weight, k_weight, v_weight
-):
-    head = key_rows.shape[1]
-    query_grad, kv_grads = attention_grads(
-        queries, key_rows, value_rows, out_grad, doc_ids.reshape(1, -1), n_ctx)
-    key_grad, value_grad = kv_grads[:, :head], kv_grads[:, head:]
-    input_grad = project_back(query_grad, q_weight) + project_back(key_grad, k_weight)
-    input_grad = (input_grad + project_back(value_grad, v_weight)).astype(BF16)
-    kv_weight_grad = lax.psum_scatter(
-        lax.dot_general(hidden, kv_grads, (((0,), (0,)), ((), ())), preferred_element_type=F32),
-        ("dp", "ctx"),
-        scatter_dimension=0,
-        tiled=True,
-    )
-    return (input_grad, kv_weight_grad)
+    )(queries, key_rows, value_rows, out_grad, doc_ids.reshape(1, -1),
+      hidden, q_weight, k_weight, v_weight)
 
 
 def solution(mesh):

time: 733 us -> 84.7 us (0.12)
  waiting for transfers between devices: 648 us -> 0 us
  Pallas kernels: 44 us -> 78.6 us
  matrix products: 17.1 us -> 0 us
  between operations: 14.1 us -> 0.65 us
    unnamed x2 -> x0, waiting for transfers between devices: 648 us -> none
    pallas_call x1, Pallas kernels: 44 us -> 78.6 us  [on_device(): pl.pallas_call(functools.partial(backward_kernel, tok * n_ctx), out_shape...]
    dot_general x4 -> x0, matrix products: 17.1 us -> none  [the longest x3 10.4 us: project_back(): lax.dot_general(grad_rows, weight, (((1,), (1,)), ((), ())), preferred_el...]
  transfers between devices with their start and end apart: 1 -> 0, of which waited for: 1 -> 0; matrix products, arithmetic and copies ran while one was open for 1% -> 0% of each run, Pallas kernels for 0% -> 0%
where the time goes in v2:
time: 84.7 us; the launch traced here: 84.6 us
  Pallas kernels  78.6 us (93%)
  local copies, waits for them, and re-layouts  5.3 us (6%)
    pallas_call x1, Pallas kernels, on_device(): pl.pallas_call(functools.partial(backward_kernel, tok * n_ctx), out_shape...  78.6 us
    unnamed x4, local copies, waits for them, and re-layouts  5.3 us

profile of v2, /device:TPU:0, one launch (start us, length us, event | category | flops | bytes accessed | tf_op | source)
XLA Modules:
  0.0 84.6 jit_solution(15551178923510976199)
XLA Ops:
  0.6 78.6 %shard_map.104 = (bf16[256,8192]{1,0:T(8,128)(2,1)}, f32[64,256]{1,0:T(8,128)}) custom-call(bf16[256,512]{1,0:T(8,128)(2,1)} %q_ref.1, bf16[256,128]{1,0:T(8,128)(2,1)} %k_ref.1, bf16[256,128]{1,0:T(8,128)(2,1)} %v_ref.1, bf16[256,512]{1,0:T(8,128)(2,1)} %do_ref.1, s32[1,256]{1,0:T(1,128)} %bitcast.1, bf16[256,8192]{1,0:T(8,128)(2,1)} %hidden_ref.1, ...), custom_call_target="tpu_custom_call" | custom-call | tf_op jit(solution)/shard_map/pallas_call | solution.py:338
  79.2 0.0 copy-start
  79.3 4.7 %copy.13 = bf16[256,8192]{1,0:T(8,128)(2,1)} copy(bf16[256,8192]{1,0:T(8,128)(2,1)} %get-tuple-element.4) | data formatting | bytes 8388608
  83.9 0.0 copy-done
  83.9 0.6 copy.14
Async XLA Ops:
  79.2 4.7 %copy-start = (f32[64,256]{1,0:T(8,128)S(1)}, f32[64,256]{1,0:T(8,128)}, u32[]{:S(2)}) copy-start(f32[64,256]{1,0:T(8,128)} %get-tuple-element.5) | copy-start | bytes 196612

commit v3 on v2

--- a/solution.py
+++ b/solution.py
@@ -23,16 +23,16 @@
 
 
 def backward_kernel(
-    seq, q_ref, k_ref, v_ref, do_ref, docs_ref, hidden_ref, qw_ref, kw_ref, vw_ref,
-    grad_ref, wgrad_ref,
-    kv, q_t, do_t, probs, max_at, run_max, run_sum, out_t, delta, dq_t, acc,
+    seq, q_hbm, k_hbm, v_hbm, do_hbm, docs_hbm, hidden_ref, qw_ref, kw_ref, vw_ref,
+    wide, wgrad_ref,
+    q_ref, k_ref, v_ref, do_ref, docs_ref, kv, q_t, do_t, probs, max_at, run_max, run_sum, out_t, delta, dq_t, acc,
     pair_out, pair_in, far_out, far_in,
-    wide, hidden_t, hidden_in, qw, kw, vw, dq, dkv,
+    hidden_t, hidden_in, qw, kw, vw, dq, dkv,
     sum1_x, sum1_y, sum1_z, got1_x, got1_y, got1_z,
     sum2_x, sum2_y, sum2_z, got2_x, got2_y, got2_z,
     sum3_x, sum3_y, sum3_z, got3_x, got3_y, got3_z,
     kv_send, kv_relay, kv_recv, pair_send, pair_recv, far_send, far_recv,
-    load_sem, store_sem, core_send, core_recv, ring_send, ring_recv,
+    load_sem, core_send, core_recv, ring_send, ring_recv,
 ):
     tok, head = k_ref.shape
     heads = q_ref.shape[1] // head
@@ -52,13 +52,24 @@
         x, y, z = [lax.rem(p + step, 4) if i == axis else p for i, p in enumerate(place)]
         return ((y % 2) * 4 + x, z * 4 + (y // 2) * 2 + core)
 
+    barrier = pltpu.get_barrier_semaphore()
+    for step in range(1, chips):
+        peer = lax.rem(chip + step, chips) * 2 + core
+        pl.semaphore_signal(barrier, inc=1, device_id=at(peer), device_id_type=MESH)
+    pl.semaphore_signal(barrier, inc=1, device_id=at(partner), device_id_type=MESH)
+    for axis, step in ((0, 1), (0, 2), (0, 3), (1, 1), (1, 3)):
+        pl.semaphore_signal(barrier, inc=1, device_id=along(axis, step), device_id_type=MESH)
+
     loads = [
         pltpu.make_async_copy(src, dst, load_sem.at[i])
-        for i, (src, dst) in enumerate(
-            ((hidden_ref, wide), (qw_ref, qw), (kw_ref, kw), (vw_ref, vw)))
+        for i, (src, dst) in enumerate((
+            (k_hbm, k_ref), (v_hbm, v_ref), (docs_hbm, docs_ref), (q_hbm, q_ref), (do_hbm, do_ref),
+            (hidden_ref, wide), (qw_ref, qw), (kw_ref, kw), (vw_ref, vw)))
     ]
     for load in loads:
         load.start()
+    for load in loads[:3]:
+        load.wait()
 
     kv[me, 0:tok, 0:head] = k_ref[...]
     kv[me, 0:tok, head : 2 * head] = v_ref[...]
@@ -68,15 +79,6 @@
     kv[me, tok : tok + 16, :] = jnp.where(digit == 0, high, low).astype(F32).astype(BF16)
     own_docs = last.astype(F32)
 
-    barrier = pltpu.get_barrier_semaphore()
-    for step in range(1, chips):
-        peer = lax.rem(chip + step, chips) * 2 + core
-        pl.semaphore_signal(barrier, inc=1, device_id=at(peer), device_id_type=MESH)
-    pl.semaphore_signal(barrier, inc=1, device_id=at(partner), device_id_type=MESH)
-    for axis, step in ((0, 1), (0, 2), (0, 3), (1, 1), (1, 3)):
-        pl.semaphore_signal(barrier, inc=1, device_id=along(axis, step), device_id_type=MESH)
-    pl.semaphore_wait(barrier, chips + 5)
-
     def kv_copy(slot, send_sem, target):
         return pltpu.make_async_remote_copy(
             src_ref=kv.at[slot], dst_ref=kv.at[slot], send_sem=send_sem,
@@ -92,25 +94,30 @@
             src_ref=far_out.at[index], dst_ref=far_in.at[slot], send_sem=far_send.at[index],
             recv_sem=far_recv.at[slot], device_id=at(index * 2 + core), device_id_type=MESH)
 
-    @pl.when(core == 0)
-    def _():
-        kv_copy(me, kv_send.at[chip], partner).start()
-
-    @pl.loop(chip + 1, chips)
-    def _(target):
-        kv_copy(me, kv_send.at[target], target * 2 + core).start()
-
+    for load in loads[3:5]:
+        load.wait()
     for h in range(heads):
         cols = slice(h * head, (h + 1) * head)
         rows = slice(h * tok, (h + 1) * tok)
         q_t[:, rows] = q_ref[:, cols].T
         do_t[:, rows] = do_ref[:, cols].T
+    pl.semaphore_wait(barrier, chips + 5)
+
+    @pl.when(core == 0)
+    def _():
+        kv_copy(me, kv_send.at[chip], partner).start()
+
+    @pl.loop(0, chips - 1 - chip)
+    def _(i):
+        target = chips - 1 - i
+        kv_copy(me, kv_send.at[target], target * 2 + core).start()
+
     run_max[...] = jnp.full_like(run_max, MASKED)
     run_sum[...] = jnp.zeros_like(run_sum)
     out_t[...] = jnp.zeros_like(out_t)
     dq_t[...] = jnp.zeros_like(dq_t)
 
-    loads[0].wait()
+    loads[5].wait()
 
     @pl.loop(0, hidden_t.shape[0])
     def _(group):
@@ -127,6 +134,7 @@
     def _(i):
         back, second = i // 2, i % 2
         source = chip - back
+        source = jnp.where((chip >= 6) & (source < 4), (source + 2) % 4, source)
         slot = 2 * source + jnp.where(second == 0, core, other)
         skipped = (i == 1) & (core == 0)
 
@@ -256,22 +264,17 @@
         for step in (2, 1, 3):
             ring_copy(0, part, step).start()
 
-    for load in loads[1:]:
+    for load in loads[6:]:
         load.wait()
     tile = 512
 
-    def store_copy(index):
-        cols = pl.ds(pl.multiple_of(index * tile, tile), tile)
-        return pltpu.make_async_copy(wide.at[:, cols], grad_ref.at[:, cols], store_sem.at[index])
-
-    @pl.loop(0, store_sem.shape[0])
+    @pl.loop(0, wide.shape[1] // tile)
     def _(index):
         rows = pl.ds(pl.multiple_of(index * tile, tile), tile)
         total = dot_rows(dq[...], qw[rows, :])
         total += dot_rows(dkv[0, :, 0:head], kw[rows, :])
         total += dot_rows(dkv[0, :, head : 2 * head], vw[rows, :])
         wide[:, rows] = total.astype(BF16)
-        store_copy(index).start()
 
     for stage in range(3):
         for part in range(3):
@@ -296,10 +299,6 @@
             for step in (1, 2, 3):
                 ring_copy(stage, part, step).wait_send()
 
-    @pl.loop(0, store_sem.shape[0])
-    def _(index):
-        store_copy(index).wait()
-
     @pl.when(core == 0)
     def _():
         kv_copy(me, kv_send.at[chip], partner).wait_send()
@@ -317,6 +316,17 @@
         kv_copy(2 * source + core, kv_relay.at[source], partner).wait_send()
         pair_copy(source).wait_send()
         far_copy(source, chip).wait_send()
+
+
+def finish_kernel(grad_ref, wgrad_ref, grad_out, wgrad_out, sem):
+    copies = [
+        pltpu.make_async_copy(grad_ref, grad_out, sem.at[0]),
+        pltpu.make_async_copy(wgrad_ref, wgrad_out, sem.at[1]),
+    ]
+    for copy in copies:
+        copy.start()
+    for copy in copies:
+        copy.wait()
 
 
 def on_device(
@@ -335,15 +345,17 @@
         for first in (lead, (3,) + lead[1:]):
             for block in ((48, head), (48, head), (16, 2 * head)):
                 sums.append(pltpu.VMEM(first + block, BF16))
-    return pl.pallas_call(
+    grads = pl.pallas_call(
         functools.partial(backward_kernel, tok * n_ctx),
-        out_shape=(
-            jax.ShapeDtypeStruct((tok, model), BF16),
-            jax.ShapeDtypeStruct((64, 2 * head), F32),
-        ),
-        in_specs=[vmem] * 5 + [hbm] * 4,
-        out_specs=(hbm, vmem),
+        out_shape=(pltpu.VMEM((tok, model), BF16), pltpu.VMEM((64, 2 * head), F32)),
+        in_specs=[hbm] * 9,
+        out_specs=(vmem, vmem),
         scratch_shapes=[
+            pltpu.VMEM((tok, width), BF16),
+            pltpu.VMEM((tok, head), BF16),
+            pltpu.VMEM((tok, head), BF16),
+            pltpu.VMEM((tok, width), BF16),
+            pltpu.VMEM((1, tok), jnp.int32),
             pltpu.VMEM((n_ctx, tok + 16, 2 * head), BF16),
             pltpu.VMEM((head, heads * tok), BF16),
             pltpu.VMEM((head, heads * tok), BF16),
@@ -359,7 +371,6 @@
             pltpu.VMEM((chips, tok, 2 * head), BF16),
             pltpu.VMEM((chips, tok, 2 * head), BF16),
             pltpu.VMEM((chips, tok, 2 * head), BF16),
-            pltpu.VMEM((tok, model), BF16),
             pltpu.VMEM((model // 128, 2, 64, tok), BF16),
             pltpu.VMEM((model // 128, 64, tok), BF16),
             pltpu.VMEM((model, width), BF16),
@@ -370,13 +381,24 @@
         ] + sums + [
             dma((chips,)), dma((chips,)), dma((n_ctx,)),
             dma((chips,)), dma((chips,)), dma((chips,)), dma((chips,)),
-            dma((4,)), dma((model // 512,)), dma((2,)), dma((2,)), dma((3, 3, 3)), dma((3, 3, 3)),
+            dma((9,)), dma((2,)), dma((2,)), dma((3, 3, 3)), dma((3, 3, 3)),
         ],
         compiler_params=pltpu.CompilerParams(
-            collective_id=0, has_side_effects=True, vmem_limit_bytes=60 * 1024 * 1024
+            collective_id=0, has_side_effects=True, vmem_limit_bytes=56 * 1024 * 1024
         ),
     )(queries, key_rows, value_rows, out_grad, doc_ids.reshape(1, -1),
       hidden, q_weight, k_weight, v_weight)
+    return pl.pallas_call(
+        finish_kernel,
+        out_shape=(
+            jax.ShapeDtypeStruct((tok, model), BF16),
+            jax.ShapeDtypeStruct((64, 2 * head), F32),
+        ),
+        in_specs=[vmem] * 2,
+        out_specs=(hbm, hbm),
+        scratch_shapes=[dma((2,))],
+        compiler_params=pltpu.CompilerParams(vmem_limit_bytes=4 * 1024 * 1024),
+    )(*grads)
 
 
 def solution(mesh):

time: 84.7 us -> 80.8 us (0.954)
  local copies, waits for them, and re-layouts: 5.3 us -> 0 us
  Pallas kernels: 78.6 us -> 80.1 us
    unnamed x4 -> x0, local copies, waits for them, and re-layouts: 5.3 us -> none
    pallas_call x0 -> x1, Pallas kernels: none -> 2.03 us  [on_device(): pl.pallas_call(finish_kernel, out_shape=(jax.ShapeDtypeStruct((tok, model...]
where the time goes in v3:
time: 80.8 us; the launch traced here: 80.7 us
  Pallas kernels  80.1 us (99%)
    pallas_call x1, Pallas kernels, on_device(): pl.pallas_call(functools.partial(backward_kernel, tok * n_ctx), out_shape...  78.1 us
    pallas_call x1, Pallas kernels, on_device(): pl.pallas_call(finish_kernel, out_shape=(jax.ShapeDtypeStruct((tok, model...  2.03 us

profile of v3, /device:TPU:0, one launch (start us, length us, event | category | flops | bytes accessed | tf_op | source)
XLA Modules:
  0.0 80.7 jit_solution(16511826656968828753)
XLA Ops:
  0.6 78.1 %shard_map.104 = (bf16[256,8192]{1,0:T(8,128)(2,1)S(1)}, f32[64,256]{1,0:T(8,128)S(1)}) custom-call(bf16[256,512]{1,0:T(8,128)(2,1)} %q_hbm.1, bf16[256,128]{1,0:T(8,128)(2,1)} %k_hbm.1, bf16[256,128]{1,0:T(8,128)(2,1)} %v_hbm.1, bf16[256,512]{1,0:T(8,128)(2,1)} %do_hbm.1, s32[1,256]{1,0:T(1,128)} %bitcast.1, bf16[256,8192]{1,0:T(8,128)(2,1)} %hidden_ref.1, ...), custom_call_target="tpu_custom_call" | custom-call | tf_op jit(solution)/shard_map/pallas_call | solution.py:348
  78.7 2.0 %shard_map.105 = (bf16[256,8192]{1,0:T(8,128)(2,1)}, f32[64,256]{1,0:T(8,128)}) custom-call(bf16[256,8192]{1,0:T(8,128)(2,1)S(1)} %get-tuple-element.4.grad_ref, f32[64,256]{1,0:T(8,128)S(1)} %get-tuple-element.5.wgrad_ref), custom_call_target="tpu_custom_call" | custom-call | tf_op jit(solution)/shard_map/pallas_call | solution.py:391

commit v4 on v3

--- a/solution.py
+++ b/solution.py
@@ -25,7 +25,7 @@
 def backward_kernel(
     seq, q_hbm, k_hbm, v_hbm, do_hbm, docs_hbm, hidden_ref, qw_ref, kw_ref, vw_ref,
     wide, wgrad_ref,
-    q_ref, k_ref, v_ref, do_ref, docs_ref, kv, q_t, do_t, probs, max_at, run_max, run_sum, out_t, delta, dq_t, acc,
+    q_ref, k_ref, v_ref, do_ref, docs_ref, kv, q_t, do_t, probs, max_at, run_max, run_sum, score_grads, delta, dq_t, acc,
     pair_out, pair_in, far_out, far_in,
     hidden_t, hidden_in, qw, kw, vw, dq, dkv,
     sum1_x, sum1_y, sum1_z, got1_x, got1_y, got1_z,
@@ -114,21 +114,18 @@
 
     run_max[...] = jnp.full_like(run_max, MASKED)
     run_sum[...] = jnp.zeros_like(run_sum)
-    out_t[...] = jnp.zeros_like(out_t)
+    delta[...] = jnp.zeros_like(delta)
     dq_t[...] = jnp.zeros_like(dq_t)
 
-    loads[5].wait()
-
-    @pl.loop(0, hidden_t.shape[0])
-    def _(group):
-        turned = wide[:, pl.ds(pl.multiple_of(group * 128, 128), 128)].T
-        hidden_t[group, 0] = turned[0:64]
-        hidden_t[group, 1] = turned[64:128]
-
-    hidden_copy = pltpu.make_async_remote_copy(
-        src_ref=hidden_t.at[:, other], dst_ref=hidden_in, send_sem=core_send.at[0],
-        recv_sem=core_recv.at[0], device_id=at(partner), device_id_type=MESH)
-    hidden_copy.start()
+    pieces = 16
+    piece_groups = hidden_t.shape[0] // pieces
+
+    def hidden_copy(piece):
+        groups = pl.ds(piece * piece_groups, piece_groups)
+        return pltpu.make_async_remote_copy(
+            src_ref=hidden_t.at[groups, other], dst_ref=hidden_in.at[groups],
+            send_sem=core_send.at[piece], recv_sem=core_recv.at[piece],
+            device_id=at(partner), device_id_type=MESH)
 
     @pl.loop(0, 2 * (chip + 1))
     def _(i):
@@ -149,7 +146,7 @@
         @pl.when(jnp.logical_not(skipped))
         def _():
             keys = kv[slot, 0:tok, 0:head]
-            values_t = kv[slot, 0:tok, head : 2 * head].T
+            values = kv[slot, 0:tok, head : 2 * head]
             digits = kv[slot, tok : tok + 16, :].astype(F32)
             key_docs = digits[0:1, :] * 64.0 + digits[1:2, :]
             key_docs = jnp.broadcast_to(key_docs, (tok, tok)).T
@@ -168,14 +165,31 @@
                 max_at[slot, :, rows] = new_max
                 run_sum[:, rows] = run_sum[:, rows] * shrink + jnp.sum(weights, axis=0, keepdims=True)
                 probs[slot, :, rows] = weights
-                out_t[:, rows] = out_t[:, rows] * shrink + dot(values_t, weights.astype(BF16))
+                prob_grad = dot(values, do_t[:, rows])
+                delta[:, rows] = delta[:, rows] * shrink + jnp.sum(
+                    weights * prob_grad, axis=0, keepdims=True)
+
+        @pl.when(i == 0)
+        def _():
+            loads[5].wait()
+
+            @pl.loop(0, hidden_t.shape[0])
+            def _(group):
+                turned = wide[:, pl.ds(pl.multiple_of(group * 128, 128), 128)].T
+                hidden_t[group, 0] = turned[0:64]
+                hidden_t[group, 1] = turned[64:128]
 
     run_sum[...] = 1.0 / run_sum[...]
-    delta[...] = run_sum[...] * jnp.sum(out_t[...] * do_t[...].astype(F32), axis=0, keepdims=True)
+    delta[...] = delta[...] * run_sum[...]
 
     @pl.loop(0, 2 * (chip + 1))
     def _(i):
-        source, second = i // 2, i % 2
+        turn, second = i // 2, i % 2
+        third = turn % 3
+        spread = jnp.where(third == 0, 2, (third - 1) * 4) + turn // 3
+        paired = (turn % 2) * 2 + turn // 2
+        source = jnp.where((chip >= 6) & (turn < 6), spread,
+                           jnp.where((chip // 2 == 2) & (turn < 4), paired, turn))
         slot = 2 * source + jnp.where(second == 0, other, core)
         own_chip = source == chip
         skipped = own_chip & (second == 0) & (core == 0)
@@ -195,7 +209,8 @@
                 score_grad = (scale * prob * (prob_grad - delta[:, rows])).astype(BF16)
                 value_part += dot(prob.astype(BF16), do_ref[:, cols])
                 key_part += dot(score_grad, q_ref[:, cols])
-                dq_t[:, rows] += dot(keys_t, score_grad)
+                score_grads[:, rows] = score_grad
+            dq_t[...] += dot(keys_t, score_grads[...])
             acc[:, 0:head] = key_part
             acc[:, head : 2 * head] = value_part
 
@@ -209,6 +224,12 @@
             pair_copy(source).wait_recv()
             far_out[source] = (acc[...] + pair_in[source].astype(F32)).astype(BF16)
             far_copy(source, chip).start()
+
+        hidden_copy(i).start()
+
+    @pl.loop(2 * (chip + 1), pieces)
+    def _(piece):
+        hidden_copy(piece).start()
 
     for h in range(heads):
         cols = slice(h * head, (h + 1) * head)
@@ -227,8 +248,8 @@
 
     dkv[0] = acc[...].astype(BF16)
     dkv_copy = pltpu.make_async_remote_copy(
-        src_ref=dkv.at[0], dst_ref=dkv.at[1], send_sem=core_send.at[1],
-        recv_sem=core_recv.at[1], device_id=at(partner), device_id_type=MESH)
+        src_ref=dkv.at[0], dst_ref=dkv.at[1], send_sem=core_send.at[pieces],
+        recv_sem=core_recv.at[pieces], device_id=at(partner), device_id_type=MESH)
     dkv_copy.start()
 
     orders = ((0, 1, 2), (1, 2, 0), (2, 0, 1))
@@ -244,7 +265,10 @@
             recv_sem=ring_recv.at[stage, part, step - 1],
             device_id=along(axis, step), device_id_type=MESH)
 
-    hidden_copy.wait_recv()
+    @pl.loop(0, pieces)
+    def _(piece):
+        hidden_copy(piece).wait_recv()
+
     dkv_copy.wait_recv()
     for step in (2, 1, 3, 0):
         x = lax.rem(place[0] + step, 4)
@@ -292,7 +316,10 @@
                 wgrad_ref[(slice(0, 48), slice(0, 48), slice(48, 64))[part],
                           (slice(0, head), slice(head, 2 * head), slice(0, 2 * head))[part]] = total
 
-    hidden_copy.wait_send()
+    @pl.loop(0, pieces)
+    def _(piece):
+        hidden_copy(piece).wait_send()
+
     dkv_copy.wait_send()
     for stage in range(3):
         for part in range(3):
@@ -363,7 +390,7 @@
             pltpu.VMEM((n_ctx, 1, heads * tok), F32),
             pltpu.VMEM((1, heads * tok), F32),
             pltpu.VMEM((1, heads * tok), F32),
-            pltpu.VMEM((head, heads * tok), F32),
+            pltpu.VMEM((tok, heads * tok), BF16),
             pltpu.VMEM((1, heads * tok), F32),
             pltpu.VMEM((head, heads * tok), F32),
             pltpu.VMEM((tok, 2 * head), F32),
@@ -381,7 +408,7 @@
         ] + sums + [
             dma((chips,)), dma((chips,)), dma((n_ctx,)),
             dma((chips,)), dma((chips,)), dma((chips,)), dma((chips,)),
-            dma((9,)), dma((2,)), dma((2,)), dma((3, 3, 3)), dma((3, 3, 3)),
+            dma((9,)), dma((17,)), dma((17,)), dma((3, 3, 3)), dma((3, 3, 3)),
         ],
         compiler_params=pltpu.CompilerParams(
             collective_id=0, has_side_effects=True, vmem_limit_bytes=56 * 1024 * 1024

time: 80.8 us -> 77.7 us (0.962)
  Pallas kernels: 80.1 us -> 77 us
    pallas_call x1, Pallas kernels: 78.1 us -> 74.9 us  [on_device(): pl.pallas_call(functools.partial(backward_kernel, tok * n_ctx), out_shape...]
where the time goes in v4:
time: 77.7 us; the launch traced here: 77.6 us
  Pallas kernels  77 us (99%)
    pallas_call x1, Pallas kernels, on_device(): pl.pallas_call(functools.partial(backward_kernel, tok * n_ctx), out_shape...  74.9 us
    pallas_call x1, Pallas kernels, on_device(): pl.pallas_call(finish_kernel, out_shape=(jax.ShapeDtypeStruct((tok, model...  2.03 us

profile of v4, /device:TPU:0, one launch (start us, length us, event | category | flops | bytes accessed | tf_op | source)
XLA Modules:
  0.0 77.6 jit_solution(12104436608496251799)
XLA Ops:
  0.6 74.9 %shard_map.104 = (bf16[256,8192]{1,0:T(8,128)(2,1)S(1)}, f32[64,256]{1,0:T(8,128)S(1)}) custom-call(bf16[256,512]{1,0:T(8,128)(2,1)} %q_hbm.1, bf16[256,128]{1,0:T(8,128)(2,1)} %k_hbm.1, bf16[256,128]{1,0:T(8,128)(2,1)} %v_hbm.1, bf16[256,512]{1,0:T(8,128)(2,1)} %do_hbm.1, s32[1,256]{1,0:T(1,128)} %bitcast.1, bf16[256,8192]{1,0:T(8,128)(2,1)} %hidden_ref.1, ...), custom_call_target="tpu_custom_call" | custom-call | tf_op jit(solution)/shard_map/pallas_call | solution.py:375
  75.6 2.0 %shard_map.105 = (bf16[256,8192]{1,0:T(8,128)(2,1)}, f32[64,256]{1,0:T(8,128)}) custom-call(bf16[256,8192]{1,0:T(8,128)(2,1)S(1)} %get-tuple-element.4.grad_ref, f32[64,256]{1,0:T(8,128)S(1)} %get-tuple-element.5.wgrad_ref), custom_call_target="tpu_custom_call" | custom-call | tf_op jit(solution)/shard_map/pallas_call | solution.py:418

commit v5 on v4

--- a/solution.py
+++ b/solution.py
@@ -25,7 +25,7 @@
 def backward_kernel(
     seq, q_hbm, k_hbm, v_hbm, do_hbm, docs_hbm, hidden_ref, qw_ref, kw_ref, vw_ref,
     wide, wgrad_ref,
-    q_ref, k_ref, v_ref, do_ref, docs_ref, kv, q_t, do_t, probs, max_at, run_max, run_sum, score_grads, delta, dq_t, acc,
+    q_ref, k_ref, v_ref, do_ref, docs_ref, kv, q_t, do_t, probs, max_at, run_max, run_sum, score_grads, delta, dq_t, parts,
     pair_out, pair_in, far_out, far_in,
     hidden_t, hidden_in, qw, kw, vw, dq, dkv,
     sum1_x, sum1_y, sum1_z, got1_x, got1_y, got1_z,
@@ -129,11 +129,13 @@
 
     @pl.loop(0, 2 * (chip + 1))
     def _(i):
-        back, second = i // 2, i % 2
+        last_step = i == 2 * chip + 1
+        second = jnp.where(last_step | ((i > 0) & (i % 2 == 0)), 1, 0)
+        back = jnp.where(last_step, chip, jnp.where(second == 1, i // 2 - 1, (i + 1) // 2))
         source = chip - back
         source = jnp.where((chip >= 6) & (source < 4), (source + 2) % 4, source)
         slot = 2 * source + jnp.where(second == 0, core, other)
-        skipped = (i == 1) & (core == 0)
+        skipped = (back == 0) & (second == 1) & (core == 0)
 
         @pl.when((i > 0) & jnp.logical_not(skipped))
         def _():
@@ -182,14 +184,16 @@
     run_sum[...] = 1.0 / run_sum[...]
     delta[...] = delta[...] * run_sum[...]
 
+    def target_of(turn):
+        across = (chip + 1) // 2
+        own_side = chip % 2
+        return jnp.where(turn == chip, chip, jnp.where(
+            turn < across, 2 * turn + 1 - own_side, 2 * (turn - across) + own_side))
+
     @pl.loop(0, 2 * (chip + 1))
     def _(i):
         turn, second = i // 2, i % 2
-        third = turn % 3
-        spread = jnp.where(third == 0, 2, (third - 1) * 4) + turn // 3
-        paired = (turn % 2) * 2 + turn // 2
-        source = jnp.where((chip >= 6) & (turn < 6), spread,
-                           jnp.where((chip // 2 == 2) & (turn < 4), paired, turn))
+        source = target_of(turn)
         slot = 2 * source + jnp.where(second == 0, other, core)
         own_chip = source == chip
         skipped = own_chip & (second == 0) & (core == 0)
@@ -211,19 +215,20 @@
                 key_part += dot(score_grad, q_ref[:, cols])
                 score_grads[:, rows] = score_grad
             dq_t[...] += dot(keys_t, score_grads[...])
-            acc[:, 0:head] = key_part
-            acc[:, head : 2 * head] = value_part
+            parts[second, :, 0:head] = key_part
+            parts[second, :, head : 2 * head] = value_part
 
         @pl.when((second == 0) & jnp.logical_not(skipped))
         def _():
-            pair_out[source] = acc[...].astype(BF16)
+            pair_out[source] = parts[0].astype(BF16)
             pair_copy(source).start()
 
-        @pl.when((second == 1) & jnp.logical_not(own_chip))
-        def _():
-            pair_copy(source).wait_recv()
-            far_out[source] = (acc[...] + pair_in[source].astype(F32)).astype(BF16)
-            far_copy(source, chip).start()
+        @pl.when((second == 0) & (turn > 0))
+        def _():
+            before = target_of(turn - 1)
+            pair_copy(before).wait_recv()
+            far_out[before] = (parts[1] + pair_in[before].astype(F32)).astype(BF16)
+            far_copy(before, chip).start()
 
         hidden_copy(i).start()
 
@@ -239,14 +244,14 @@
     @pl.when(core == 0)
     def _():
         pair_copy(chip).wait_recv()
-        acc[...] += pair_in[chip].astype(F32)
+        parts[1] += pair_in[chip].astype(F32)
 
     @pl.loop(chip + 1, chips)
     def _(source):
         far_copy(source, source).wait_recv()
-        acc[...] += far_in[source].astype(F32)
-
-    dkv[0] = acc[...].astype(BF16)
+        parts[1] += far_in[source].astype(F32)
+
+    dkv[0] = parts[1].astype(BF16)
     dkv_copy = pltpu.make_async_remote_copy(
         src_ref=dkv.at[0], dst_ref=dkv.at[1], send_sem=core_send.at[pieces],
         recv_sem=core_recv.at[pieces], device_id=at(partner), device_id_type=MESH)
@@ -393,7 +398,7 @@
             pltpu.VMEM((tok, heads * tok), BF16),
             pltpu.VMEM((1, heads * tok), F32),
             pltpu.VMEM((head, heads * tok), F32),
-            pltpu.VMEM((tok, 2 * head), F32),
+            pltpu.VMEM((2, tok, 2 * head), F32),
             pltpu.VMEM((chips, tok, 2 * head), BF16),
             pltpu.VMEM((chips, tok, 2 * head), BF16),
             pltpu.VMEM((chips, tok, 2 * head), BF16),

time: 77.7 us -> 74.2 us (0.955)
  Pallas kernels: 77 us -> 73.4 us
    pallas_call x1, Pallas kernels: 74.9 us -> 71.4 us  [on_device(): pl.pallas_call(functools.partial(backward_kernel, tok * n_ctx), out_shape...]
where the time goes in v5:
time: 74.2 us; the launch traced here: 74 us
  Pallas kernels  73.4 us (99%)
    pallas_call x1, Pallas kernels, on_device(): pl.pallas_call(functools.partial(backward_kernel, tok * n_ctx), out_shape...  71.4 us
    pallas_call x1, Pallas kernels, on_device(): pl.pallas_call(finish_kernel, out_shape=(jax.ShapeDtypeStruct((tok, model...  2.03 us

profile of v5, /device:TPU:0, one launch (start us, length us, event | category | flops | bytes accessed | tf_op | source)
XLA Modules:
  0.0 74.0 jit_solution(9703355677644355769)
XLA Ops:
  0.6 71.4 %shard_map.104 = (bf16[256,8192]{1,0:T(8,128)(2,1)S(1)}, f32[64,256]{1,0:T(8,128)S(1)}) custom-call(bf16[256,512]{1,0:T(8,128)(2,1)} %q_hbm.1, bf16[256,128]{1,0:T(8,128)(2,1)} %k_hbm.1, bf16[256,128]{1,0:T(8,128)(2,1)} %v_hbm.1, bf16[256,512]{1,0:T(8,128)(2,1)} %do_hbm.1, s32[1,256]{1,0:T(1,128)} %bitcast.1, bf16[256,8192]{1,0:T(8,128)(2,1)} %hidden_ref.1, ...), custom_call_target="tpu_custom_call" | custom-call | tf_op jit(solution)/shard_map/pallas_call | solution.py:380
  72.0 2.0 %shard_map.105 = (bf16[256,8192]{1,0:T(8,128)(2,1)}, f32[64,256]{1,0:T(8,128)}) custom-call(bf16[256,8192]{1,0:T(8,128)(2,1)S(1)} %get-tuple-element.4.grad_ref, f32[64,256]{1,0:T(8,128)S(1)} %get-tuple-element.5.wgrad_ref), custom_call_target="tpu_custom_call" | custom-call | tf_op jit(solution)/shard_map/pallas_call | solution.py:423

commit v6 on v5

--- a/solution.py
+++ b/solution.py
@@ -31,7 +31,7 @@
     sum1_x, sum1_y, sum1_z, got1_x, got1_y, got1_z,
     sum2_x, sum2_y, sum2_z, got2_x, got2_y, got2_z,
     sum3_x, sum3_y, sum3_z, got3_x, got3_y, got3_z,
-    kv_send, kv_relay, kv_recv, pair_send, pair_recv, far_send, far_recv,
+    kv_send, kv_relay, kv_pass, kv_recv, pair_send, pair_recv, far_send, far_recv,
     load_sem, core_send, core_recv, ring_send, ring_recv,
 ):
     tok, head = k_ref.shape
@@ -103,6 +103,24 @@
         do_t[:, rows] = do_ref[:, cols].T
     pl.semaphore_wait(barrier, chips + 5)
 
+    plane, side = chip // 2, chip % 2
+    neighbour = (2 * plane + 1 - side) * 2 + core
+    passes_on = plane >= 2
+    passed_chip = (3 - plane) * 2 + side
+
+    def sent_straight(target):
+        return (target // 2 + plane != 3) | (target % 2 == side)
+
+    def source_of(back):
+        k = back - side
+        far_plane = jnp.where((k == 1) | (k == 4), 0, jnp.where(k <= 3, 2, 1))
+        far_side = jnp.where((k == 1) | (k == 2) | (k == 5), side, 1 - side)
+        near_plane = jnp.where(k <= 2, 1, 0)
+        near_side = jnp.where(k % 2 == 1, side, 1 - side)
+        return jnp.where(
+            (k >= 1) & (plane == 3), 2 * far_plane + far_side,
+            jnp.where((k >= 1) & (plane == 2), 2 * near_plane + near_side, chip - back))
+
     @pl.when(core == 0)
     def _():
         kv_copy(me, kv_send.at[chip], partner).start()
@@ -110,7 +128,10 @@
     @pl.loop(0, chips - 1 - chip)
     def _(i):
         target = chips - 1 - i
-        kv_copy(me, kv_send.at[target], target * 2 + core).start()
+
+        @pl.when(sent_straight(target) & (target // 2 != plane + 2))
+        def _():
+            kv_copy(me, kv_send.at[target], target * 2 + core).start()
 
     run_max[...] = jnp.full_like(run_max, MASKED)
     run_sum[...] = jnp.zeros_like(run_sum)
@@ -132,8 +153,7 @@
         last_step = i == 2 * chip + 1
         second = jnp.where(last_step | ((i > 0) & (i % 2 == 0)), 1, 0)
         back = jnp.where(last_step, chip, jnp.where(second == 1, i // 2 - 1, (i + 1) // 2))
-        source = chip - back
-        source = jnp.where((chip >= 6) & (source < 4), (source + 2) % 4, source)
+        source = source_of(back)
         slot = 2 * source + jnp.where(second == 0, core, other)
         skipped = (back == 0) & (second == 1) & (core == 0)
 
@@ -144,6 +164,10 @@
         @pl.when((i > 0) & (second == 0))
         def _():
             kv_copy(slot, kv_relay.at[source], partner).start()
+
+        @pl.when((second == 0) & passes_on & (source == passed_chip))
+        def _():
+            kv_copy(slot, kv_pass.at[0], neighbour).start()
 
         @pl.when(jnp.logical_not(skipped))
         def _():
@@ -181,6 +205,13 @@
                 hidden_t[group, 0] = turned[0:64]
                 hidden_t[group, 1] = turned[64:128]
 
+            @pl.when(plane < 2)
+            def _():
+                kv_copy(me, kv_send.at[passed_chip], passed_chip * 2 + core).wait_send()
+                for target_side in range(2):
+                    target = 2 * (plane + 2) + target_side
+                    kv_copy(me, kv_send.at[target], target * 2 + core).start()
+
     run_sum[...] = 1.0 / run_sum[...]
     delta[...] = delta[...] * run_sum[...]
 
@@ -270,6 +301,15 @@
             recv_sem=ring_recv.at[stage, part, step - 1],
             device_id=along(axis, step), device_id_type=MESH)
 
+    def quarter_copy(part, step, x):
+        axis = orders[part][0]
+        return pltpu.make_async_remote_copy(
+            src_ref=sums[0][part].at[lax.rem(place[axis] + step, 4), x],
+            dst_ref=gots[0][part].at[step - 1, x],
+            send_sem=ring_send.at[0, part, step - 1],
+            recv_sem=ring_recv.at[0, part, step - 1],
+            device_id=along(axis, step), device_id_type=MESH)
+
     @pl.loop(0, pieces)
     def _(piece):
         hidden_copy(piece).wait_recv()
@@ -285,13 +325,13 @@
             for y_hi in range(2):
                 y = y_hi * 2 + y_lo
                 sum1_x[x, y] = terms[:, y_hi, 0:48, 0:head]
-                sum1_y[y, :, x] = terms[:, y_hi, 0:48, head : 2 * head]
+                sum1_y[y, x] = terms[:, y_hi, 0:48, head : 2 * head]
                 sum1_z[:, x, y] = terms[:, y_hi, 48:64, :]
         if step > 0:
             ring_copy(0, 0, step).start()
-    for part in (1, 2):
-        for step in (2, 1, 3):
-            ring_copy(0, part, step).start()
+        for part in (1, 2):
+            for away in (2, 1, 3):
+                quarter_copy(part, away, x).start()
 
     for load in loads[6:]:
         load.wait()
@@ -310,16 +350,22 @@
             for step in (1, 3, 2):
                 ring_copy(stage, part, step).wait_recv()
             mine = place[orders[part][stage]]
-            total = sums[stage][part][mine].astype(F32)
-            for step in range(3):
-                total += gots[stage][part][step].astype(F32)
-            if stage < 2:
-                sums[stage + 1][part][...] = total.astype(sums[stage + 1][part].dtype)
-                for step in (2, 1, 3):
-                    ring_copy(stage + 1, part, step).start()
-            else:
+            if stage == 2:
+                total = sums[2][part][mine].astype(F32)
+                for came in range(3):
+                    total += gots[2][part][came].astype(F32)
                 wgrad_ref[(slice(0, 48), slice(0, 48), slice(48, 64))[part],
                           (slice(0, head), slice(head, 2 * head), slice(0, 2 * head))[part]] = total
+                continue
+            for step in (2, 1, 3, 0):
+                index = lax.rem(place[orders[part][stage + 1]] + step, 4)
+                where = (slice(None), index) if (stage, part) == (0, 1) else (index,)
+                total = sums[stage][part][(mine,) + where].astype(F32)
+                for came in range(3):
+                    total += gots[stage][part][(came,) + where].astype(F32)
+                sums[stage + 1][part][index] = total.astype(BF16)
+                if step > 0:
+                    ring_copy(stage + 1, part, step).start()
 
     @pl.loop(0, pieces)
     def _(piece):
@@ -341,7 +387,13 @@
 
     @pl.loop(chip + 1, chips)
     def _(target):
-        kv_copy(me, kv_send.at[target], target * 2 + core).wait_send()
+        @pl.when(sent_straight(target) & ((plane >= 2) | (target != passed_chip)))
+        def _():
+            kv_copy(me, kv_send.at[target], target * 2 + core).wait_send()
+
+    @pl.when(passes_on)
+    def _():
+        kv_copy(2 * passed_chip + core, kv_pass.at[0], neighbour).wait_send()
 
     @pl.loop(0, chip)
     def _(source):
@@ -411,7 +463,7 @@
             pltpu.VMEM((tok, width), BF16),
             pltpu.VMEM((2, tok, 2 * head), BF16),
         ] + sums + [
-            dma((chips,)), dma((chips,)), dma((n_ctx,)),
+            dma((chips,)), dma((chips,)), dma((1,)), dma((n_ctx,)),
             dma((chips,)), dma((chips,)), dma((chips,)), dma((chips,)),
             dma((9,)), dma((17,)), dma((17,)), dma((3, 3, 3)), dma((3, 3, 3)),
         ],

time: 74.2 us -> 71.1 us (0.958)
  Pallas kernels: 73.4 us -> 70.1 us
    pallas_call x1, Pallas kernels: 71.4 us -> 68 us  [on_device(): pl.pallas_call(functools.partial(backward_kernel, tok * n_ctx), out_shape...]
where the time goes in v6:
time: 71.1 us; the launch traced here: 70.7 us
  Pallas kernels  70.1 us (99%)
    pallas_call x1, Pallas kernels, on_device(): pl.pallas_call(functools.partial(backward_kernel, tok * n_ctx), out_shape...  68 us
    pallas_call x1, Pallas kernels, on_device(): pl.pallas_call(finish_kernel, out_shape=(jax.ShapeDtypeStruct((tok, model...  2.03 us

profile of v6, /device:TPU:0, one launch (start us, length us, event | category | flops | bytes accessed | tf_op | source)
XLA Modules:
  0.0 70.7 jit_solution(4321783350100257570)
XLA Ops:
  0.6 68.0 %shard_map.104 = (bf16[256,8192]{1,0:T(8,128)(2,1)S(1)}, f32[64,256]{1,0:T(8,128)S(1)}) custom-call(bf16[256,512]{1,0:T(8,128)(2,1)} %q_hbm.1, bf16[256,128]{1,0:T(8,128)(2,1)} %k_hbm.1, bf16[256,128]{1,0:T(8,128)(2,1)} %v_hbm.1, bf16[256,512]{1,0:T(8,128)(2,1)} %do_hbm.1, s32[1,256]{1,0:T(1,128)} %bitcast.1, bf16[256,8192]{1,0:T(8,128)(2,1)} %hidden_ref.1, ...), custom_call_target="tpu_custom_call" | custom-call | tf_op jit(solution)/shard_map/pallas_call | solution.py:432
  68.7 2.0 %shard_map.105 = (bf16[256,8192]{1,0:T(8,128)(2,1)}, f32[64,256]{1,0:T(8,128)}) custom-call(bf16[256,8192]{1,0:T(8,128)(2,1)S(1)} %get-tuple-element.4.grad_ref, f32[64,256]{1,0:T(8,128)S(1)} %get-tuple-element.5.wgrad_ref), custom_call_target="tpu_custom_call" | custom-call | tf_op jit(solution)/shard_map/pallas_call | solution.py:475

commit v7 on v6

--- a/solution.py
+++ b/solution.py
@@ -26,12 +26,12 @@
     seq, q_hbm, k_hbm, v_hbm, do_hbm, docs_hbm, hidden_ref, qw_ref, kw_ref, vw_ref,
     wide, wgrad_ref,
     q_ref, k_ref, v_ref, do_ref, docs_ref, kv, q_t, do_t, probs, max_at, run_max, run_sum, score_grads, delta, dq_t, parts,
-    pair_out, pair_in, far_out, far_in,
+    pair_out, pair_in, far_out, far_in, joined,
     hidden_t, hidden_in, qw, kw, vw, dq, dkv,
     sum1_x, sum1_y, sum1_z, got1_x, got1_y, got1_z,
     sum2_x, sum2_y, sum2_z, got2_x, got2_y, got2_z,
     sum3_x, sum3_y, sum3_z, got3_x, got3_y, got3_z,
-    kv_send, kv_relay, kv_pass, kv_recv, pair_send, pair_recv, far_send, far_recv,
+    kv_send, kv_relay, kv_pass, kv_recv, pair_send, pair_recv, far_send, far_recv, join_sem,
     load_sem, core_send, core_recv, ring_send, ring_recv,
 ):
     tok, head = k_ref.shape
@@ -219,7 +219,12 @@
         across = (chip + 1) // 2
         own_side = chip % 2
         return jnp.where(turn == chip, chip, jnp.where(
-            turn < across, 2 * turn + 1 - own_side, 2 * (turn - across) + own_side))
+            turn < across, 2 * turn + 1 - own_side, 2 * (chip - 1 - turn) + own_side))
+
+    def join_copy():
+        return pltpu.make_async_remote_copy(
+            src_ref=far_out.at[1 - side], dst_ref=joined, send_sem=join_sem.at[0],
+            recv_sem=join_sem.at[1], device_id=at(neighbour), device_id_type=MESH)
 
     @pl.loop(0, 2 * (chip + 1))
     def _(i):
@@ -258,8 +263,21 @@
         def _():
             before = target_of(turn - 1)
             pair_copy(before).wait_recv()
+
+            @pl.when((plane >= 2) & (before == side))
+            def _():
+                join_copy().wait_recv()
+                parts[1] += joined[...].astype(F32)
+
             far_out[before] = (parts[1] + pair_in[before].astype(F32)).astype(BF16)
-            far_copy(before, chip).start()
+
+            @pl.when((plane >= 2) & (before == 1 - side))
+            def _():
+                join_copy().start()
+
+            @pl.when((plane < 2) | (before != 1 - side))
+            def _():
+                far_copy(before, chip).start()
 
         hidden_copy(i).start()
 
@@ -279,8 +297,10 @@
 
     @pl.loop(chip + 1, chips)
     def _(source):
-        far_copy(source, source).wait_recv()
-        parts[1] += far_in[source].astype(F32)
+        @pl.when((plane > 0) | (source < 4) | (source % 2 == side))
+        def _():
+            far_copy(source, source).wait_recv()
+            parts[1] += far_in[source].astype(F32)
 
     dkv[0] = parts[1].astype(BF16)
     dkv_copy = pltpu.make_async_remote_copy(
@@ -314,14 +334,22 @@
     def _(piece):
         hidden_copy(piece).wait_recv()
 
+    for step in range(4):
+        x = lax.rem(place[0] + step, 4)
+        for y_lo in range(2):
+            own = hidden_t[pl.ds(y_lo * 32 + x * 8, 8), core].reshape(512, tok)
+            own_terms = dot(own, dkv[0])
+            probs[2 * step + y_lo, :, 0 : 2 * head] = own_terms[0:256]
+            probs[2 * step + y_lo, :, 2 * head : 4 * head] = own_terms[256:512]
     dkv_copy.wait_recv()
     for step in (2, 1, 3, 0):
         x = lax.rem(place[0] + step, 4)
         for y_lo in range(2):
-            groups = pl.ds(y_lo * 32 + x * 8, 8)
-            own = hidden_t[groups, core].reshape(512, tok)
-            paired = hidden_in[groups].reshape(512, tok)
-            terms = (dot(own, dkv[0]) + dot(paired, dkv[1])).astype(BF16).reshape(4, 2, 64, 2 * head)
+            paired = hidden_in[pl.ds(y_lo * 32 + x * 8, 8)].reshape(512, tok)
+            own_terms = jnp.concatenate(
+                [probs[2 * step + y_lo, :, 0 : 2 * head],
+                 probs[2 * step + y_lo, :, 2 * head : 4 * head]], axis=0)
+            terms = (own_terms + dot(paired, dkv[1])).astype(BF16).reshape(4, 2, 64, 2 * head)
             for y_hi in range(2):
                 y = y_hi * 2 + y_lo
                 sum1_x[x, y] = terms[:, y_hi, 0:48, 0:head]
@@ -399,7 +427,14 @@
     def _(source):
         kv_copy(2 * source + core, kv_relay.at[source], partner).wait_send()
         pair_copy(source).wait_send()
-        far_copy(source, chip).wait_send()
+
+        @pl.when((plane < 2) | (source != 1 - side))
+        def _():
+            far_copy(source, chip).wait_send()
+
+    @pl.when(plane >= 2)
+    def _():
+        join_copy().wait_send()
 
 
 def finish_kernel(grad_ref, wgrad_ref, grad_out, wgrad_out, sem):
@@ -455,6 +490,7 @@
             pltpu.VMEM((chips, tok, 2 * head), BF16),
             pltpu.VMEM((chips, tok, 2 * head), BF16),
             pltpu.VMEM((chips, tok, 2 * head), BF16),
+            pltpu.VMEM((tok, 2 * head), BF16),
             pltpu.VMEM((model // 128, 2, 64, tok), BF16),
             pltpu.VMEM((model // 128, 64, tok), BF16),
             pltpu.VMEM((model, width), BF16),
@@ -464,7 +500,7 @@
             pltpu.VMEM((2, tok, 2 * head), BF16),
         ] + sums + [
             dma((chips,)), dma((chips,)), dma((1,)), dma((n_ctx,)),
-            dma((chips,)), dma((chips,)), dma((chips,)), dma((chips,)),
+            dma((chips,)), dma((chips,)), dma((chips,)), dma((chips,)), dma((2,)),
             dma((9,)), dma((17,)), dma((17,)), dma((3, 3, 3)), dma((3, 3, 3)),
         ],
         compiler_params=pltpu.CompilerParams(

time: 71.1 us -> 70.3 us (0.989)
  Pallas kernels: 70.1 us -> 69.2 us
    pallas_call x1, Pallas kernels: 68 us -> 67.2 us  [on_device(): pl.pallas_call(functools.partial(backward_kernel, tok * n_ctx), out_shape...]
where the time goes in v7:
time: 70.3 us; the launch traced here: 69.8 us
  Pallas kernels  69.2 us (98%)
    pallas_call x1, Pallas kernels, on_device(): pl.pallas_call(functools.partial(backward_kernel, tok * n_ctx), out_shape...  67.2 us
    pallas_call x1, Pallas kernels, on_device(): pl.pallas_call(finish_kernel, out_shape=(jax.ShapeDtypeStruct((tok, model...  2.03 us

profile of v7, /device:TPU:0, one launch (start us, length us, event | category | flops | bytes accessed | tf_op | source)
XLA Modules:
  0.0 69.8 jit_solution(5926310208158313161)
XLA Ops:
  0.6 67.2 %shard_map.104 = (bf16[256,8192]{1,0:T(8,128)(2,1)S(1)}, f32[64,256]{1,0:T(8,128)S(1)}) custom-call(bf16[256,512]{1,0:T(8,128)(2,1)} %q_hbm.1, bf16[256,128]{1,0:T(8,128)(2,1)} %k_hbm.1, bf16[256,128]{1,0:T(8,128)(2,1)} %v_hbm.1, bf16[256,512]{1,0:T(8,128)(2,1)} %do_hbm.1, s32[1,256]{1,0:T(1,128)} %bitcast.1, bf16[256,8192]{1,0:T(8,128)(2,1)} %hidden_ref.1, ...), custom_call_target="tpu_custom_call" | custom-call | tf_op jit(solution)/shard_map/pallas_call | solution.py:467
  67.8 2.0 %shard_map.105 = (bf16[256,8192]{1,0:T(8,128)(2,1)}, f32[64,256]{1,0:T(8,128)}) custom-call(bf16[256,8192]{1,0:T(8,128)(2,1)S(1)} %get-tuple-element.4.grad_ref, f32[64,256]{1,0:T(8,128)S(1)} %get-tuple-element.5.wgrad_ref), custom_call_target="tpu_custom_call" | custom-call | tf_op jit(solution)/shard_map/pallas_call | solution.py:511

commit v8 on v7

--- a/solution.py
+++ b/solution.py
@@ -31,7 +31,7 @@
     sum1_x, sum1_y, sum1_z, got1_x, got1_y, got1_z,
     sum2_x, sum2_y, sum2_z, got2_x, got2_y, got2_z,
     sum3_x, sum3_y, sum3_z, got3_x, got3_y, got3_z,
-    kv_send, kv_relay, kv_pass, kv_recv, pair_send, pair_recv, far_send, far_recv, join_sem,
+    kv_send, kv_relay, kv_pass, kv_recv, pair_send, pair_recv, far_send, far_recv, join_send, join_recv,
     load_sem, core_send, core_recv, ring_send, ring_recv,
 ):
     tok, head = k_ref.shape
@@ -218,13 +218,19 @@
     def target_of(turn):
         across = (chip + 1) // 2
         own_side = chip % 2
+        later = turn - across
+        own_plane = jnp.where(plane == 3, jnp.where(later == 0, 2, later - 1), plane - 1 - later)
         return jnp.where(turn == chip, chip, jnp.where(
-            turn < across, 2 * turn + 1 - own_side, 2 * (chip - 1 - turn) + own_side))
-
-    def join_copy():
-        return pltpu.make_async_remote_copy(
-            src_ref=far_out.at[1 - side], dst_ref=joined, send_sem=join_sem.at[0],
-            recv_sem=join_sem.at[1], device_id=at(neighbour), device_id_type=MESH)
+            turn < across, 2 * turn + 1 - own_side, 2 * own_plane + own_side))
+
+    def joins(target):
+        return target // 2 < plane - 1
+
+    def join_copy(index):
+        return pltpu.make_async_remote_copy(
+            src_ref=far_out.at[2 * index + 1 - side], dst_ref=joined.at[index],
+            send_sem=join_send.at[index], recv_sem=join_recv.at[index],
+            device_id=at(neighbour), device_id_type=MESH)
 
     @pl.loop(0, 2 * (chip + 1))
     def _(i):
@@ -264,18 +270,18 @@
             before = target_of(turn - 1)
             pair_copy(before).wait_recv()
 
-            @pl.when((plane >= 2) & (before == side))
+            @pl.when(joins(before) & (before % 2 == side))
             def _():
-                join_copy().wait_recv()
-                parts[1] += joined[...].astype(F32)
+                join_copy(before // 2).wait_recv()
+                parts[1] += joined[before // 2].astype(F32)
 
             far_out[before] = (parts[1] + pair_in[before].astype(F32)).astype(BF16)
 
-            @pl.when((plane >= 2) & (before == 1 - side))
+            @pl.when(joins(before) & (before % 2 != side))
             def _():
-                join_copy().start()
-
-            @pl.when((plane < 2) | (before != 1 - side))
+                join_copy(before // 2).start()
+
+            @pl.when(jnp.logical_not(joins(before)) | (before % 2 == side))
             def _():
                 far_copy(before, chip).start()
 
@@ -297,7 +303,7 @@
 
     @pl.loop(chip + 1, chips)
     def _(source):
-        @pl.when((plane > 0) | (source < 4) | (source % 2 == side))
+        @pl.when((plane >= source // 2 - 1) | (source % 2 == side))
         def _():
             far_copy(source, source).wait_recv()
             parts[1] += far_in[source].astype(F32)
@@ -428,13 +434,13 @@
         kv_copy(2 * source + core, kv_relay.at[source], partner).wait_send()
         pair_copy(source).wait_send()
 
-        @pl.when((plane < 2) | (source != 1 - side))
+        @pl.when(jnp.logical_not(joins(source)) | (source % 2 == side))
         def _():
             far_copy(source, chip).wait_send()
 
-    @pl.when(plane >= 2)
-    def _():
-        join_copy().wait_send()
+    @pl.loop(0, jnp.maximum(plane - 1, 0))
+    def _(index):
+        join_copy(index).wait_send()
 
 
 def finish_kernel(grad_ref, wgrad_ref, grad_out, wgrad_out, sem):
@@ -490,7 +496,7 @@
             pltpu.VMEM((chips, tok, 2 * head), BF16),
             pltpu.VMEM((chips, tok, 2 * head), BF16),
             pltpu.VMEM((chips, tok, 2 * head), BF16),
-            pltpu.VMEM((tok, 2 * head), BF16),
+            pltpu.VMEM((2, tok, 2 * head), BF16),
             pltpu.VMEM((model // 128, 2, 64, tok), BF16),
             pltpu.VMEM((model // 128, 64, tok), BF16),
             pltpu.VMEM((model, width), BF16),
@@ -500,7 +506,7 @@
             pltpu.VMEM((2, tok, 2 * head), BF16),
         ] + sums + [
             dma((chips,)), dma((chips,)), dma((1,)), dma((n_ctx,)),
-            dma((chips,)), dma((chips,)), dma((chips,)), dma((chips,)), dma((2,)),
+            dma((chips,)), dma((chips,)), dma((chips,)), dma((chips,)), dma((2,)), dma((2,)),
             dma((9,)), dma((17,)), dma((17,)), dma((3, 3, 3)), dma((3, 3, 3)),
         ],
         compiler_params=pltpu.CompilerParams(

time: 70.3 us -> 69.1 us (0.983)
  Pallas kernels: 69.2 us -> 68.3 us
    pallas_call x1, Pallas kernels: 67.2 us -> 66.3 us  [on_device(): pl.pallas_call(functools.partial(backward_kernel, tok * n_ctx), out_shape...]
where the time goes in v8:
time: 69.1 us; the launch traced here: 69 us
  Pallas kernels  68.3 us (99%)
    pallas_call x1, Pallas kernels, on_device(): pl.pallas_call(functools.partial(backward_kernel, tok * n_ctx), out_shape...  66.3 us
    pallas_call x1, Pallas kernels, on_device(): pl.pallas_call(finish_kernel, out_shape=(jax.ShapeDtypeStruct((tok, model...  2.03 us

profile of v8, /device:TPU:0, one launch (start us, length us, event | category | flops | bytes accessed | tf_op | source)
XLA Modules:
  0.0 69.0 jit_solution(5025924526765629595)
XLA Ops:
  0.6 66.3 %shard_map.104 = (bf16[256,8192]{1,0:T(8,128)(2,1)S(1)}, f32[64,256]{1,0:T(8,128)S(1)}) custom-call(bf16[256,512]{1,0:T(8,128)(2,1)} %q_hbm.1, bf16[256,128]{1,0:T(8,128)(2,1)} %k_hbm.1, bf16[256,128]{1,0:T(8,128)(2,1)} %v_hbm.1, bf16[256,512]{1,0:T(8,128)(2,1)} %do_hbm.1, s32[1,256]{1,0:T(1,128)} %bitcast.1, bf16[256,8192]{1,0:T(8,128)(2,1)} %hidden_ref.1, ...), custom_call_target="tpu_custom_call" | custom-call | tf_op jit(solution)/shard_map/pallas_call | solution.py:473
  66.9 2.0 %shard_map.105 = (bf16[256,8192]{1,0:T(8,128)(2,1)}, f32[64,256]{1,0:T(8,128)}) custom-call(bf16[256,8192]{1,0:T(8,128)(2,1)S(1)} %get-tuple-element.4.grad_ref, f32[64,256]{1,0:T(8,128)S(1)} %get-tuple-element.5.wgrad_ref), custom_call_target="tpu_custom_call" | custom-call | tf_op jit(solution)/shard_map/pallas_call | solution.py:517
